TPU v7x, 128 devices: a whole 4x4x4 slice. The times are simulated.
128 devices in a mesh: dp: 64 (over z_hi, y, x, core), chip: 2 (over z_lo).
Axes of the slice: x: 4, y: 4, z: 4 (z_hi: 2, z_lo: 2; z = z_hi * 2 + z_lo), core: 2. Of those that a mesh axis runs over, the one named last changes fastest.
Arguments:
- moe_in: bfloat16 [2048, 3584], P(('dp', 'chip')), may hold values from -6 to 6
- expert_ids: int32 [2048, 8], P(('dp', 'chip')), may hold values from 0 to 127, as said below
- expert_gates: float32 [2048, 8], P(('dp', 'chip')), may hold values from 0.1 to 1
- gate_weight: bfloat16 [128, 3584, 1024], P(('dp', 'chip')), may hold values from -0.09375 to 0.09375
- up_weight: bfloat16 [128, 3584, 1024], P(('dp', 'chip')), may hold values from -0.09375 to 0.09375
- down_weight: bfloat16 [128, 1024, 3584], P(('dp', 'chip')), may hold values from -0.1875 to 0.1875
- queries: bfloat16 [384, 128, 576], P(('dp', 'chip')), may hold values from -14 to 14
- cache_pool: bfloat16 [3328, 64, 576], P(('dp', 'chip')), may hold values from -4 to 4
- req_source: int32 [384], replicated, may hold values from 0 to 127, as said below
- req_first: int32 [384], replicated, may hold values from 0 to 14, as said below
- req_tokens: int32 [384], replicated, may hold values from 1 to 768, as said below
Outputs:
- moe_out: bfloat16 [2048, 3584], P(('dp', 'chip'))
- attn_latent: bfloat16 [384, 128, 512], P(('dp', 'chip'))
Inputs may be any that keep to these rules, and one draw needn't show every extreme that they name: `expert_ids`: expert e belongs to rank e. Each row names 8 different experts; the rows of one rank name any one expert at most 2 times; in every draw one expert is named exactly 2 times by the rows of every rank. `req_source`: request r is served by rank r // 3. Its source is that rank or one of the 1 ranks before it, cyclically; a rank serves exactly 1 request whose source lies k ranks before it, for each k from 1 to 1. `req_first`: A request's blocks lie contiguously in its source rank's 26 blocks. A rank's blocks for the requests it serves itself fill exactly its first 14 blocks; those for the request served k ranks after it fill exactly blocks 26 - (2 - k) * 12 up to 26 - (1 - k) * 12, so the request served 1 ranks after its source starts at block 14. `req_tokens`: A request has ceil(length / 64) blocks, at most 12; every rank serves a request of 768 tokens.
All inputs are finite; a program needn't handle non-finite values.
Results may differ from a plain program's by a relative error of at most 0.0058.
Values may be sent and summed in bfloat16 or wider, within the bound.
No kernel may reach another device: no remote copies, remote signals or barrier semaphores. Data moves between devices by JAX's collectives and lax.ppermute only.
A program may use at most 128 MiB of HBM per device.

v0:
```python
import math

import jax
import jax.numpy as jnp
from jax import lax
from jax.sharding import PartitionSpec as P

LATENT = 512
MAX_BLOCKS = 12
HOPS = 1
MOVE_BLOCKS = 12


score_scale = 1.0 / math.sqrt(192.0)


def from_behind(block, axis, distance):
    devices = range(lax.axis_size(axis))
    route = [((i - distance) % len(devices), i) for i in devices]
    return lax.ppermute(block, axis, route)


def attend(query_rows, cache_rows, lengths):
    scores = (
        jnp.einsum("rhd,rtd->rht", query_rows, cache_rows, preferred_element_type=jnp.float32)
        * score_scale
    )
    in_range = jnp.arange(cache_rows.shape[1])[None, None, :] < lengths[:, None, None]
    row_max = jnp.max(jnp.where(in_range, scores, -1e30), axis=-1, keepdims=True)
    weights = jnp.where(in_range, jnp.exp(scores - row_max), 0.0)
    softmax_out = (weights / jnp.sum(weights, axis=-1, keepdims=True)).astype(jnp.bfloat16)
    return jnp.einsum(
        "rht,rtc->rhc", softmax_out, cache_rows[:, :, :LATENT], preferred_element_type=jnp.float32
    ).astype(jnp.bfloat16)


def gather_blocks(blocks, first_blocks, offset):
    block_index = first_blocks[:, None] + offset[:, None] + jnp.arange(MAX_BLOCKS)[None, :]
    block_index = jnp.minimum(block_index, blocks.shape[0] - 1)
    picked = jnp.take(blocks, block_index.reshape(-1), axis=0)
    return picked.reshape(first_blocks.shape[0], MAX_BLOCKS * blocks.shape[1], blocks.shape[2])


def expert_rows(arrived, gate_weight, up_weight, down_weight):
    flat_rows = arrived.reshape(-1, arrived.shape[-1])
    gate_part = jnp.dot(flat_rows, gate_weight[0], preferred_element_type=jnp.float32)
    up_part = jnp.dot(flat_rows, up_weight[0], preferred_element_type=jnp.float32)
    hidden = (jax.nn.silu(gate_part) * up_part).astype(jnp.bfloat16)
    return (
        jnp.dot(hidden, down_weight[0], preferred_element_type=jnp.float32)
        .astype(jnp.bfloat16)
        .reshape(arrived.shape)
    )


def plan_slice(plan_table, rank_index, per_rank):
    return lax.dynamic_slice_in_dim(plan_table, rank_index * per_rank, per_rank)


def per_device(
    moe_in,
    expert_ids,
    expert_gates,
    gate_weight,
    up_weight,
    down_weight,
    queries,
    cache_pool,
    req_source,
    req_first,
    req_tokens,
):
    group_size = lax.axis_size(("dp", "chip"))
    row_count, model_width = moe_in.shape
    top_count = expert_ids.shape[1]
    capacity = 2 * row_count * top_count // group_size
    flat_ids = expert_ids.reshape(-1)
    one_hot = (flat_ids[:, None] == jnp.arange(group_size)[None, :]).astype(jnp.int32)
    position = jnp.sum((jnp.cumsum(one_hot, axis=0) - 1) * one_hot, axis=1)
    slot_ids = (flat_ids * capacity + position).reshape(row_count, top_count)
    routing = jnp.any(
        slot_ids[None, :, :] == jnp.arange(group_size * capacity)[:, None, None], axis=2
    ).astype(jnp.bfloat16)
    outgoing = jnp.dot(routing, moe_in, preferred_element_type=jnp.float32).astype(jnp.bfloat16)
    outgoing = outgoing.reshape(group_size, capacity, model_width)
    answered = expert_rows(
        lax.all_to_all(outgoing, ("dp", "chip"), split_axis=0, concat_axis=0, tiled=True),
        gate_weight,
        up_weight,
        down_weight,
    )
    returned = lax.all_to_all(answered, ("dp", "chip"), split_axis=0, concat_axis=0, tiled=True)
    returned = returned.reshape(group_size * capacity, model_width)
    picked = jnp.take(returned, slot_ids.reshape(-1), axis=0).reshape(
        row_count, top_count, model_width
    )
    moe_out = jnp.sum(expert_gates[:, :, None] * picked, axis=1).astype(jnp.bfloat16)
    my_rank = lax.axis_index(("dp", "chip"))
    per_rank = queries.shape[0]
    pool_size = cache_pool.shape[0]
    sources = plan_slice(req_source, my_rank, per_rank)
    firsts = plan_slice(req_first, my_rank, per_rank)
    lengths = plan_slice(req_tokens, my_rank, per_rank)
    hop_of = jnp.mod(my_rank - sources, group_size)
    pieces = [cache_pool]
    region_start = pool_size - (HOPS + 1 - 1) * MOVE_BLOCKS
    pieces.append(
        from_behind(cache_pool[region_start : region_start + MOVE_BLOCKS], ("dp", "chip"), 1)
    )
    available = jnp.concatenate(pieces, axis=0)
    offset = jnp.where(hop_of > 0, HOPS * MOVE_BLOCKS, 0)
    attn_latent = attend(queries, gather_blocks(available, firsts, offset), lengths)
    return (moe_out, attn_latent)


def solution(mesh):
    placed = (
        P(("dp", "chip"), None),
        P(("dp", "chip"), None),
        P(("dp", "chip"), None),
        P(("dp", "chip"), None, None),
        P(("dp", "chip"), None, None),
        P(("dp", "chip"), None, None),
        P(("dp", "chip"), None, None),
        P(("dp", "chip"), None, None),
        P(),
        P(),
        P(),
    )
    return jax.shard_map(
        per_device,
        mesh=mesh,
        in_specs=placed,
        out_specs=(P(("dp", "chip"), None), P(("dp", "chip"), None, None)),
        check_vma=False,
    )
```

profile of v0, /device:TPU:0, one launch (start us, length us, event | category | flops | bytes accessed | tf_op | source)
XLA Modules:
  0.0 115.7 jit_solution(7677962880660129906)
XLA Ops:
  0.6 0.0 copy-start
  0.6 0.8 copy.24
  1.5 0.1 reshape.142
  1.5 0.1 fusion.39
  1.6 0.2 reduce_window_sum.11
  1.8 0.2 select_reduce_fusion.1
  2.0 0.1 reduce_sum.32
  2.1 0.6 compare_and_fusion
  2.7 0.1 fusion.38
  2.8 1.6 %convolution_convert_fusion = bf16[256,3584]{1,0:T(8,128)(2,1)S(1)} fusion(pred[256,16]{0,1:T(8,128)(4,1)S(1)} %fusion.38, bf16[16,3584]{1,0:T(8,128)(2,1)} %param.11), kind=kOutput, calls=%fused_computation.10 | convolution fusion | flops 30277632 | bytes 1953792 | tf_op jit(solution)/shard_map/dot_general | solution.py:84
  4.4 1.7 %reshape.143 = bf16[128,2,3584]{2,1,0:T(2,128)(2,1)} reshape(bf16[256,3584]{1,0:T(8,128)(2,1)S(1)} %convolution_convert_fusion) | data formatting | bytes 3670016 | tf_op jit(solution)/shard_map/reshape | solution.py:85
  6.1 11.1 %all-to-all-start = ((bf16[128,2,3584]{2,1,0:T(2,128)(2,1)}), bf16[128,2,3584]{2,1,0:T(2,128)(2,1)S(1)}, u32[]{:S(2)}, u32[]{:S(2)}) async-start(bf16[128,2,3584]{2,1,0:T(2,128)(2,1)} %reshape.143), calls=%async_computation | async-start | bytes 3670016 | tf_op jit(solution)/shard_map/all_to_all | solution.py:87
  17.2 1.3 %slice.6 = bf16[12,64,576]{2,1,0:T(8,128)(2,1)S(1)} slice(bf16[26,64,576]{2,1,0:T(8,128)(2,1)} %param.18), slice={[14:26], [0:64], [0:576]} | slice | bytes 1769472 | tf_op jit(solution)/shard_map/slice | solution.py:108
  18.5 1.2 collective-permute-start
  19.7 0.8 fusion.40
  20.4 0.1 add_minimum_fusion
  20.5 0.1 min.22
  20.6 0.1 mul.60
  20.7 0.6 pad_clamp_fusion
  21.3 0.1 compare_and_fusion.1
  21.4 23.0 %all-to-all-done = bf16[128,2,3584]{2,1,0:T(2,128)(2,1)S(1)} async-done(((bf16[128,2,3584]{2,1,0:T(2,128)(2,1)}), bf16[128,2,3584]{2,1,0:T(2,128)(2,1)S(1)}, u32[]{:S(2)}, u32[]{:S(2)}) %all-to-all-start) | async-done | bytes 1835040 | tf_op jit(solution)/shard_map/all_to_all | solution.py:87
  44.4 1.7 %reshape.144 = bf16[256,3584]{1,0:T(8,128)(2,1)} reshape(bf16[128,2,3584]{2,1,0:T(2,128)(2,1)S(1)} %all-to-all-done) | data formatting | bytes 3670016 | tf_op jit(solution)/shard_map/reshape | solution.py:45
  46.1 6.8 %fusion.5 = f32[256,1024]{1,0:T(8,128)} fusion(bf16[256,3584]{1,0:T(8,128)(2,1)} %reshape.144, bf16[1,3584,1024]{2,1,0:T(8,128)(2,1)} %param.14), kind=kOutput, calls=%fused_computation.7 | convolution fusion | flops 1879048192 | bytes 10223616 | tf_op jit(solution)/shard_map/dot_general | solution.py:46
  52.9 0.0 copy-done.1
  52.9 10.8 %fusion.7 = bf16[256,3584]{1,0:T(8,128)(2,1)} fusion(bf16[1,1024,3584]{2,1,0:T(8,128)(2,1)} %param.16, bf16[256,3584]{1,0:T(8,128)(2,1)S(1)} %copy-done.1, bf16[1,3584,1024]{2,1,0:T(8,128)(2,1)} %param.15, f32[256,1024]{1,0:T(8,128)} %fusion.5), kind=kOutput, calls=%fused_computation.9 | convolution fusion | flops 3760586752 | bytes 19398656 | tf_op jit(solution)/shard_map/dot_general | solution.py:50
  63.7 4.7 %reshape.145 = bf16[128,2,3584]{2,1,0:T(2,128)(2,1)} reshape(bf16[256,3584]{1,0:T(8,128)(2,1)} %fusion.7) | data formatting | bytes 3670016 | tf_op jit(solution)/shard_map/reshape | solution.py:52
  68.4 13.9 %all-to-all-start.1 = ((bf16[128,2,3584]{2,1,0:T(2,128)(2,1)}), bf16[128,2,3584]{2,1,0:T(2,128)(2,1)}, u32[]{:S(2)}, u32[]{:S(2)}) async-start(bf16[128,2,3584]{2,1,0:T(2,128)(2,1)} %reshape.145), calls=%async_computation.1 | async-start | bytes 3670016 | tf_op jit(solution)/shard_map/all_to_all | solution.py:92
  82.3 0.6 pad_clamp_fusion.1
  82.9 0.1 broadcast_in_dim.62
  83.0 0.7 broadcast_in_dim.63
  83.7 0.8 dynamic_slice.9
  84.4 0.0 copy-done.5
  84.4 0.7 copy.23
  85.1 0.7 iota_compare_fusion.2
  85.8 0.0 collective-permute-done
  85.8 2.3 %pad_maximum_fusion = bf16[38,64,576]{2,1,0:T(8,128)(2,1)S(1)} fusion(bf16[12,64,576]{2,1,0:T(8,128)(2,1)} %collective-permute-done, bf16[26,64,576]{2,1,0:T(8,128)(2,1)} %param.18), kind=kLoop, calls=%fused_computation.11 | loop fusion | flops 1400832 | bytes 5603328 | tf_op jit(solution)/shard_map/concatenate | solution.py:110
  88.1 2.9 %gather_fusion.1 = bf16[36,64,576]{2,1,0:T(8,128)(2,1)} fusion(bf16[38,64,576]{2,1,0:T(8,128)(2,1)S(1)} %pad_maximum_fusion, s32[1024]{0:T(1024)} %pad_clamp_fusion), kind=kCustom, calls=%fused_computation.1 | custom fusion | bytes 5308560 | tf_op jit(solution)/shard_map/jit(_take)/gather | solution.py:40
  91.0 2.1 %bitcast_select_fusion = bf16[3,768,576]{2,1,0:T(8,128)(2,1)S(1)} fusion(pred[3,768]{1,0:T(4,128)(4,1)} %broadcast_in_dim.63, bf16[3,768,576]{2,1,0:T(8,128)(2,1)} %bitcast.40), kind=kLoop, calls=%fused_computation.12 | loop fusion | flops 1327104 | bytes 5310720 | tf_op jit(solution)/shard_map/jit(_take)/select_n | solution.py:40
  93.2 0.0 copy-done
  93.2 0.0 copy-start.3
  93.2 0.9 convolution_multiply_fusion
  94.1 0.9 fusion.48
  95.0 1.3 %fusion.29 = bf16[3,128,512]{2,1,0:T(8,128)(2,1)} fusion(bf16[3,768,576]{2,1,0:T(8,128)(2,1)S(1)} %bitcast_select_fusion, f32[3,128,768]{1,2,0:T(8,128)S(1)} %get-tuple-element.5, f32[3,128]{1,0:T(4,128)S(1)} %get-tuple-element.4), kind=kOutput, calls=%fused_computation.25 | convolution fusion | flops 302776320 | bytes 3934208 | tf_op jit(solution)/shard_map/rht,rtc->rhc/dot_general | solution.py:32
  96.3 12.6 %all-to-all-done.1 = bf16[128,2,3584]{2,1,0:T(2,128)(2,1)} async-done(((bf16[128,2,3584]{2,1,0:T(2,128)(2,1)}), bf16[128,2,3584]{2,1,0:T(2,128)(2,1)}, u32[]{:S(2)}, u32[]{:S(2)}) %all-to-all-start.1) | async-done | bytes 1835040 | tf_op jit(solution)/shard_map/all_to_all | solution.py:92
  109.0 4.1 %reshape.146 = bf16[256,3584]{1,0:T(8,128)(2,1)S(1)} reshape(bf16[128,2,3584]{2,1,0:T(2,128)(2,1)} %all-to-all-done.1) | data formatting | bytes 3670016 | tf_op jit(solution)/shard_map/reshape | solution.py:93
  113.0 0.0 copy-start.2
  113.0 1.2 %gather_fusion = bf16[128,3584]{1,0:T(8,128)(2,1)S(1)} fusion(bf16[256,3584]{1,0:T(8,128)(2,1)S(1)} %reshape.146, s32[1024]{0:T(1024)} %pad_clamp_fusion.1), kind=kCustom, calls=%fused_computation | custom fusion | bytes 1835520 | tf_op jit(solution)/shard_map/jit(_take)/gather | solution.py:94
  114.3 1.4 %multiply_reduce_fusion = bf16[16,3584]{1,0:T(8,128)(2,1)} fusion(bf16[128,3584]{1,0:T(8,128)(2,1)S(1)} %gather_fusion, f32[16,8]{1,0:T(8,128)S(1)} %copy-done.2, pred[16,8]{1,0:T(8,128)(4,1)S(1)} %copy-done.4), kind=kLoop, calls=%fused_computation.15 | loop fusion | flops 1777664 | bytes 1032832 | tf_op jit(solution)/shard_map/reduce_sum | solution.py:97
  (9 shorter events, 0.0 us)
Async XLA Ops:
  0.6 92.5 %copy-start = (bf16[3,128,576]{1,2,0:T(8,128)(2,1)S(1)}, bf16[3,128,576]{1,2,0:T(8,128)(2,1)}, u32[]{:S(2)}) copy-start(bf16[3,128,576]{1,2,0:T(8,128)(2,1)} %param.17) | copy-start | bytes 1327108
  6.1 38.3 %all-to-all-start = ((bf16[128,2,3584]{2,1,0:T(2,128)(2,1)}), bf16[128,2,3584]{2,1,0:T(2,128)(2,1)S(1)}, u32[]{:S(2)}, u32[]{:S(2)}) async-start(bf16[128,2,3584]{2,1,0:T(2,128)(2,1)} %reshape.143), calls=%async_computation | async-start | bytes 3670016 | tf_op jit(solution)/shard_map/all_to_all | solution.py:87
  18.5 67.3 %collective-permute-start = (bf16[12,64,576]{2,1,0:T(8,128)(2,1)S(1)}, bf16[12,64,576]{2,1,0:T(8,128)(2,1)}, u32[]{:S(2)}, u32[]{:S(2)}) collective-permute-start(bf16[12,64,576]{2,1,0:T(8,128)(2,1)S(1)} %slice.6), channel_id=1, source_target_pairs={{127,0},{0,1},{1,2},{2,3},{3,4},{4,5},{5,6},{6,7},{7,8},{8,9},{9,1... | collective-permute-start | bytes 2654216 | tf_op jit(solution)/shard_map/ppermute | solution.py:20
  46.1 6.8 %copy-start.1 = (bf16[256,3584]{1,0:T(8,128)(2,1)S(1)}, bf16[256,3584]{1,0:T(8,128)(2,1)}, u32[]{:S(2)}) copy-start(bf16[256,3584]{1,0:T(8,128)(2,1)} %reshape.144) | copy-start | bytes 5505028
  68.4 16.0 %copy-start.5 = (f32[16,8]{0,1:T(8,128)S(1)}, f32[16,8]{0,1:T(8,128)}, u32[]{:S(2)}) copy-start(f32[16,8]{0,1:T(8,128)} %param.13) | copy-start | bytes 1540
  68.4 40.5 %all-to-all-start.1 = ((bf16[128,2,3584]{2,1,0:T(2,128)(2,1)}), bf16[128,2,3584]{2,1,0:T(2,128)(2,1)}, u32[]{:S(2)}, u32[]{:S(2)}) async-start(bf16[128,2,3584]{2,1,0:T(2,128)(2,1)} %reshape.145), calls=%async_computation.1 | async-start | bytes 3670016 | tf_op jit(solution)/shard_map/all_to_all | solution.py:92
  93.2 0.9 copy-start.3
  113.0 1.3 %copy-start.2 = (f32[16,8]{1,0:T(8,128)S(1)}, f32[16,8]{1,0:T(8,128)}, u32[]{:S(2)}) copy-start(f32[16,8]{1,0:T(8,128)} %copy.23) | copy-start | bytes 1540
  113.0 1.3 %copy-start.4 = (pred[16,8]{1,0:T(8,128)(4,1)S(1)}, pred[16,8]{1,0:T(8,128)(4,1)}, u32[]{:S(2)}) copy-start(pred[16,8]{1,0:T(8,128)(4,1)} %get-tuple-element.2) | copy-start | bytes 388
where the time goes:
time: 116 us
  waiting for transfers between devices  35.6 us (31%)
  starting transfers between devices  26.2 us (23%)
  matrix products  21.4 us (18%)
  local copies, waits for them, and re-layouts  21 us (18%)
  other arithmetic  10.7 us (9%)
    all_to_all x1, waiting for transfers between devices, per_device(): lax.all_to_all(outgoing, ('dp', 'chip'), split_axis=0, concat_axis=0, til...  23 us
    all_to_all x1, starting transfers between devices, per_device(): lax.all_to_all(answered, ('dp', 'chip'), split_axis=0, concat_axis=0, til...  13.9 us
    all_to_all x1, waiting for transfers between devices, per_device(): lax.all_to_all(answered, ('dp', 'chip'), split_axis=0, concat_axis=0, til...  12.6 us
    all_to_all x1, starting transfers between devices, per_device(): lax.all_to_all(outgoing, ('dp', 'chip'), split_axis=0, concat_axis=0, til...  11.1 us
    dot_general x1, matrix products, expert_rows(): jnp.dot(hidden, down_weight[0], preferred_element_type=jnp.float32)  10.8 us
    dot_general x1, matrix products, expert_rows(): jnp.dot(flat_rows, gate_weight[0], preferred_element_type=jnp.float32)  6.82 us
    reshape x1, local copies, waits for them, and re-layouts, expert_rows(): return jnp.dot(hidden, down_weight[0], preferred_element_type=jnp.float32...  4.75 us
    reshape x1, local copies, waits for them, and re-layouts, per_device(): returned = returned.reshape(group_size * capacity, model_width)  4.06 us
  transfers between devices with their start and end apart: 3, of which 2 were waited for; matrix products, arithmetic and copies ran while one was open for 35% of the time, Pallas kernels for 0%

commit v1 on v0

v1 whole, which is shorter than its diff:
```python
import math

import jax
import jax.numpy as jnp
from jax import lax
from jax.experimental import pallas as pl
from jax.experimental.pallas import tpu as pltpu
from jax.sharding import PartitionSpec as P

LATENT = 512
MAX_BLOCKS = 12
POOL = 26
REQUESTS = 3
SLOTS = 2
PARTS = 4
LANES = 128
MIB = 1 << 20
STEP = 256

score_scale = 1.0 / math.sqrt(192.0)

VMEM = pl.BlockSpec(memory_space=pltpu.VMEM)
SMEM = pl.BlockSpec(memory_space=pltpu.SMEM)
HBM = pl.BlockSpec(memory_space=pltpu.HBM)
AXES = ("dp", "chip")


def call(kernel, out_shape, in_specs, out_specs, scratch=(), limit=24 * MIB, aliases={}):
    return pl.pallas_call(
        kernel,
        out_shape=out_shape,
        in_specs=in_specs,
        out_specs=out_specs,
        scratch_shapes=scratch,
        input_output_aliases=aliases,
        compiler_params=pltpu.CompilerParams(vmem_limit_bytes=limit),
    )


def dot(a, b, contract=((1,), (0,))):
    return lax.dot_general(a, b, (contract, ((), ())), preferred_element_type=jnp.float32)


def moved_at(source_ref, rank, per_rank):
    first = rank * per_rank
    at = jnp.int32(0)
    for i in range(1, per_rank):
        at = jnp.where(source_ref[first + i] != rank, i, at)
    return at


def iota(shape, dim):
    return lax.broadcasted_iota(jnp.int32, shape, dim)


def send_kernel(source_hbm, ids_hbm, x_hbm, queries_hbm, out_hbm, query_ref, source_ref, ids_ref, x_ref, queries_ref, out_ref, sems):
    pairs = ((ids_hbm, ids_ref), (x_hbm, x_ref), (source_hbm, source_ref), (queries_hbm, queries_ref))
    fetches = [pltpu.make_async_copy(here, there, sems.at[i]) for i, (here, there) in enumerate(pairs)]
    for fetch in fetches:
        fetch.start()
    top, rows = ids_ref.shape
    messages, piece = out_ref.shape
    place_count = SLOTS * PARTS
    ranks = messages // place_count
    columns = PARTS * rows
    shape = (columns, columns)
    before = (iota(shape, 0) // rows == iota(shape, 1) // rows) & (iota(shape, 0) < iota(shape, 1))
    before = before.astype(jnp.bfloat16)
    expert = iota((ranks, columns), 0)
    fetches[0].wait()
    ids = jnp.concatenate([ids_ref[...]] * PARTS, axis=1)
    named = jnp.zeros((ranks, columns), jnp.float32)
    for k in range(top):
        named += (ids[k : k + 1, :] == expert).astype(jnp.float32)
    named = named.astype(jnp.bfloat16)
    slot = jnp.where(named > 0, dot(named, before), -1.0).astype(jnp.bfloat16)
    fetches[1].wait()
    pieces = jnp.concatenate([x_ref[:, p * piece : (p + 1) * piece] for p in range(PARTS)], axis=0)
    steps = 4
    step = messages // steps
    sends = []
    for n in range(steps):
        at = n * step
        spread = ((iota((step, ranks), 0) + at) // place_count == iota((step, ranks), 1)).astype(jnp.bfloat16)
        place = iota((step, columns), 0) % place_count
        hit = (dot(spread, slot) == (place // PARTS).astype(jnp.float32)) & (place % PARTS == iota((step, columns), 1) // rows)
        out_ref[at : at + step, :] = dot(hit.astype(jnp.bfloat16), pieces).astype(jnp.bfloat16)
        sends.append(pltpu.make_async_copy(out_ref.at[pl.ds(at, step)], out_hbm.at[pl.ds(at, step)], sems.at[4 + n]))
        sends[-1].start()
    fetches[2].wait()
    fetches[3].wait()
    query_ref[...] = queries_ref[moved_at(source_ref, lax.axis_index(AXES), REQUESTS)]
    for send in sends:
        send.wait()


def attend(query_cols, cache_rows, length):
    scores = dot(cache_rows, query_cols) * score_scale
    in_range = iota(scores.shape, 0) < length
    row_max = jnp.max(jnp.where(in_range, scores, -1e30), axis=0, keepdims=True)
    weights = jnp.where(in_range, jnp.exp(scores - row_max), 0.0)
    softmax_out = (weights / jnp.sum(weights, axis=0, keepdims=True)).astype(jnp.bfloat16)
    return dot(softmax_out, cache_rows[:, :LATENT], ((0,), (0,))).astype(jnp.bfloat16)


def spread_gates(ids_ref, gates_ref, out_ref):
    rows, top = ids_ref.shape
    messages = out_ref.shape[1]
    place_count = SLOTS * PARTS
    ranks = messages // place_count
    expert = iota((rows, ranks), 1)
    named = jnp.zeros((rows, ranks), jnp.float32)
    rest = jnp.zeros((rows, ranks), jnp.float32)
    for k in range(top):
        chosen = ids_ref[:, k : k + 1] == expert
        named += chosen.astype(jnp.float32)
        rest += jnp.where(chosen, gates_ref[:, k : k + 1], 0.0)
    before = (iota((rows, rows), 1) < iota((rows, rows), 0)).astype(jnp.bfloat16)
    slot = jnp.where(named > 0, dot(before, named.astype(jnp.bfloat16)), -1.0)
    shape = (ranks, messages)
    spread = (iota(shape, 1) // place_count == iota(shape, 0)).astype(jnp.bfloat16)
    place = iota((rows, messages), 1) % place_count
    hit = dot(slot.astype(jnp.bfloat16), spread) == (place // PARTS).astype(jnp.float32)
    for third in range(3):
        head = rest.astype(jnp.bfloat16)
        rest = rest - head.astype(jnp.float32)
        spread_head = jnp.where(hit, dot(head, spread), 0.0)
        for p in range(PARTS):
            at = (third * PARTS + p) * rows
            out_ref[at : at + rows, :] = jnp.where(place % PARTS == p, spread_head, 0.0).astype(jnp.bfloat16)


def window(cache_ref, first):
    block_rows = cache_ref.shape[0] // POOL
    start = pl.multiple_of(first * block_rows, block_rows)
    return cache_ref[pl.ds(start, MAX_BLOCKS * block_rows), :]


def own_kernel(source_ref, first_ref, tokens_ref, queries_ref, cache_ref, ids_ref, gates_ref, attn_ref, spread_ref):
    spread_gates(ids_ref, gates_ref, spread_ref)
    my_rank = lax.axis_index(AXES)
    mine = moved_at(source_ref, my_rank, REQUESTS)
    for r in (jnp.where(mine == 0, 1, 0), jnp.where(mine == 2, 1, 2)):
        n = my_rank * REQUESTS + r
        attn_ref[r] = attend(queries_ref[r], window(cache_ref, first_ref[n]), tokens_ref[n])
    attn_ref[mine] = jnp.zeros(attn_ref.shape[1:], attn_ref.dtype)


def moved_kernel(source_ref, first_ref, tokens_ref, query_ref, cache_ref, out_ref):
    next_rank = lax.rem(lax.axis_index(AXES) + 1, source_ref.shape[0] // REQUESTS)
    n = next_rank * REQUESTS + moved_at(source_ref, next_rank, REQUESTS)
    out_ref[...] = attend(query_ref[...], window(cache_ref, first_ref[n]), tokens_ref[n])


def expert_kernel(x_ref, gate_hbm, up_hbm, down_hbm, out_ref, gate_ref, up_ref, down_ref, wide, flat, hidden, sems):
    messages, piece = x_ref.shape
    units = hidden.shape[1]
    place_count = SLOTS * PARTS
    ranks = messages // place_count
    strips = piece // LANES
    count = 0

    def fetch(here, there, at, width):
        nonlocal count
        columns = pl.ds(at, width)
        copy = pltpu.make_async_copy(here.at[:, columns], there.at[:, columns], sems.at[count])
        copy.start()
        count += 1
        return copy

    near = [(fetch(gate_hbm, gate_ref, n, STEP), fetch(up_hbm, up_ref, n, STEP)) for n in range(0, units, STEP)]
    lows = range(0, piece, STEP)
    far = [[fetch(down_hbm, down_ref, p * piece + low, min(STEP, piece - low)) for p in range(PARTS)] for low in lows]
    for c in range(strips):
        wide[c] = x_ref[:, c * LANES : (c + 1) * LANES].astype(jnp.float32)
    for place in range(place_count):
        s, p = divmod(place, PARTS)
        for c in range(strips):
            at = p * piece + c * LANES
            taken = wide[c, pl.ds(place, ranks, stride=place_count), :]
            flat[s * ranks : (s + 1) * ranks, at : at + LANES] = taken.astype(jnp.bfloat16)
    for n, group in zip(range(0, units, STEP), near):
        for copy in group:
            copy.wait()
        gate_part = dot(flat[...], gate_ref[:, n : n + STEP])
        up_part = dot(flat[...], up_ref[:, n : n + STEP])
        hidden[:, n : n + STEP] = (gate_part / (1.0 + jnp.exp(-gate_part)) * up_part).astype(jnp.bfloat16)
    for low, group in zip(lows, far):
        high = min(low + STEP, piece)
        for copy in group:
            copy.wait()
        for p in range(PARTS):
            result = dot(hidden[...], down_ref[:, p * piece + low : p * piece + high])
            for s in range(SLOTS):
                for c in range(low // LANES, high // LANES):
                    at = c * LANES - low
                    kept = result[s * ranks : (s + 1) * ranks, at : at + LANES]
                    wide[c, pl.ds(s * PARTS + p, ranks, stride=place_count), :] = kept
        for c in range(low // LANES, high // LANES):
            out_ref[:, c * LANES : (c + 1) * LANES] = wide[c].astype(jnp.bfloat16)


def combine_kernel(source_ref, gates_ref, returned_ref, moved_hbm, attn_hbm, out_ref, attn_out_hbm, sem):
    del attn_hbm
    my_rank = lax.axis_index(AXES)
    mine = moved_at(source_ref, my_rank, REQUESTS)
    copy = pltpu.make_async_copy(moved_hbm, attn_out_hbm.at[mine], sem)
    copy.start()
    rows = out_ref.shape[0]
    piece = returned_ref.shape[1]
    total = dot(gates_ref[...], returned_ref[...])
    for p in range(PARTS):
        thirds = [total[(third * PARTS + p) * rows : (third * PARTS + p + 1) * rows] for third in range(3)]
        out_ref[:, p * piece : (p + 1) * piece] = (thirds[0] + thirds[1] + thirds[2]).astype(jnp.bfloat16)
    copy.wait()


def per_device(
    moe_in,
    expert_ids,
    expert_gates,
    gate_weight,
    up_weight,
    down_weight,
    queries,
    cache_pool,
    req_source,
    req_first,
    req_tokens,
):
    group_size = lax.axis_size(AXES)
    row_count, model_width = moe_in.shape
    place_count = SLOTS * PARTS
    messages = group_size * place_count
    piece = model_width // PARTS
    units = gate_weight.shape[2]
    heads, features = queries.shape[1:]
    bf16 = jnp.bfloat16
    dma = pltpu.SemaphoreType.DMA

    def exchange(x):
        x = x.reshape(group_size, place_count, piece)
        return lax.all_to_all(x, AXES, split_axis=0, concat_axis=0, tiled=True).reshape(messages, piece)

    def to_rank(x, distance):
        return lax.ppermute(x, AXES, [(i, (i + distance) % group_size) for i in range(group_size)])

    def stay(*arrays):
        return [pltpu.with_memory_space_constraint(x, pltpu.HBM) for x in arrays]

    message = (messages, piece)
    query_cols = jnp.swapaxes(queries, 1, 2)
    outgoing, moved_query = call(
        send_kernel,
        (pltpu.HBM(message, bf16), jax.ShapeDtypeStruct((features, heads), bf16)),
        [HBM] * 4,
        (HBM, VMEM),
        [
            pltpu.SMEM(req_source.shape, jnp.int32),
            pltpu.VMEM(expert_ids.shape[::-1], jnp.int32),
            pltpu.VMEM(moe_in.shape, bf16),
            pltpu.VMEM(query_cols.shape, bf16),
            pltpu.VMEM(message, bf16),
            dma((8,)),
        ],
    )(*stay(req_source, expert_ids.T, moe_in, query_cols))
    moved_query = to_rank(moved_query, -1)
    arrived = exchange(outgoing)

    cache_rows = cache_pool.reshape(-1, features)
    plan = (req_source, req_first, req_tokens)
    attn_own, gates = call(
        own_kernel,
        (
            jax.ShapeDtypeStruct((REQUESTS, heads, LATENT), bf16),
            jax.ShapeDtypeStruct((3 * PARTS * row_count, messages), bf16),
        ),
        [SMEM] * 3 + [VMEM] * 4,
        (VMEM,) * 2,
    )(*plan, query_cols, cache_rows, expert_ids, expert_gates)
    moved_out = call(moved_kernel, jax.ShapeDtypeStruct((heads, LATENT), bf16), [SMEM] * 3 + [VMEM] * 2, VMEM)(
        *plan, moved_query, cache_rows
    )
    arrived, moved_out, attn_own, gates = lax.optimization_barrier((arrived, moved_out, attn_own, gates))
    moved_out = to_rank(moved_out, 1)
    answered = call(
        expert_kernel,
        jax.ShapeDtypeStruct(message, bf16),
        [VMEM] + [HBM] * 3,
        VMEM,
        [
            pltpu.VMEM(gate_weight.shape[1:], bf16),
            pltpu.VMEM(up_weight.shape[1:], bf16),
            pltpu.VMEM(down_weight.shape[1:], bf16),
            pltpu.VMEM((piece // LANES, messages, LANES), jnp.float32),
            pltpu.VMEM((SLOTS * group_size, model_width), bf16),
            pltpu.VMEM((SLOTS * group_size, units), bf16),
            dma((2 * (units // STEP) + PARTS * -(-piece // STEP),)),
        ],
        limit=44 * MIB,
    )(arrived, *stay(gate_weight[0], up_weight[0], down_weight[0]))
    answered, moved_out = lax.optimization_barrier((answered, moved_out))
    returned = exchange(answered)
    moe_out, attn_latent = call(
        combine_kernel,
        (jax.ShapeDtypeStruct(moe_in.shape, bf16), jax.ShapeDtypeStruct(attn_own.shape, bf16)),
        [SMEM, VMEM, VMEM, HBM, HBM],
        (VMEM, HBM),
        [dma],
        aliases={4: 1},
    )(req_source, gates, returned, moved_out, attn_own)
    return (moe_out, attn_latent)


def solution(mesh):
    rows = P(("dp", "chip"), None)
    blocks = P(("dp", "chip"), None, None)
    return jax.shard_map(
        per_device,
        mesh=mesh,
        in_specs=(rows, rows, rows, blocks, blocks, blocks, blocks, blocks, P(), P(), P()),
        out_specs=(rows, blocks),
        check_vma=False,
    )
```

time: 116 us -> 93.4 us (0.81)
  blocking collectives: 0 us -> 36.1 us
  Pallas kernels: 0 us -> 22.3 us
  waiting for transfers between devices: 35.6 us -> 14.2 us
  matrix products: 21.4 us -> 0 us
  local copies, waits for them, and re-layouts: 21 us -> 0.17 us
  other arithmetic: 10.7 us -> 0 us
  starting transfers between devices: 26.2 us -> 19.5 us
    all_to_all x0 -> x1, blocking collectives: none -> 36.1 us  [exchange(): lax.all_to_all(x, AXES, split_axis=0, concat_axis=0, tiled=True)]
    all_to_all x2 -> x1, waiting for transfers between devices: 35.6 us -> 1.51 us  [exchange(): lax.all_to_all(x, AXES, split_axis=0, concat_axis=0, tiled=True)]
    pallas_call x0 -> x5, Pallas kernels: none -> 22.3 us  [the longest x1 11.6 us: per_device(): call(expert_kernel, jax.ShapeDtypeStruct(message, bf16), [VMEM] + [HBM] *...]
    dot_general x5 -> x0, matrix products: 21.4 us -> none  [the longest x1 10.8 us: expert_rows(): jnp.dot(hidden, down_weight[0], preferred_element_type=jnp.float32)]
    all_to_all x2 -> x1, starting transfers between devices: 25 us -> 11.6 us  [exchange(): lax.all_to_all(x, AXES, split_axis=0, concat_axis=0, tiled=True)]
    ppermute x1 -> x2, waiting for transfers between devices: 0.01 us -> 12.7 us  [to_rank(): lax.ppermute(x, AXES, [(i, (i + distance) % group_size) for i in range(gr...]
    reshape x5 -> x0, local copies, waits for them, and re-layouts: 12.2 us -> none  [the longest x1 4.75 us: expert_rows(): return jnp.dot(hidden, down_weight[0], preferred_element_type=jnp.float32...]
    ppermute x1 -> x2, starting transfers between devices: 1.16 us -> 7.9 us  [to_rank(): lax.ppermute(x, AXES, [(i, (i + distance) % group_size) for i in range(gr...]
  transfers between devices with their start and end apart: 3 -> 3, of which waited for: 2 -> 2; matrix products, arithmetic and copies ran while one was open for 35% -> 0% of each run, Pallas kernels for 0% -> 18%
where the time goes in v1:
time: 93.4 us; the launch traced here: 93 us
  blocking collectives  36.1 us (39%)
  Pallas kernels  22.3 us (24%)
  starting transfers between devices  19.5 us (21%)
  waiting for transfers between devices  14.2 us (15%)
    all_to_all x1, blocking collectives, exchange(): lax.all_to_all(x, AXES, split_axis=0, concat_axis=0, tiled=True)  36.1 us
    ppermute x2, waiting for transfers between devices, to_rank(): lax.ppermute(x, AXES, [(i, (i + distance) % group_size) for i in range(gr...  12.7 us
    all_to_all x1, starting transfers between devices, exchange(): lax.all_to_all(x, AXES, split_axis=0, concat_axis=0, tiled=True)  11.6 us
    pallas_call x1, Pallas kernels, per_device(): call(expert_kernel, jax.ShapeDtypeStruct(message, bf16), [VMEM] + [HBM] *...  11.6 us
    ppermute x2, starting transfers between devices, to_rank(): lax.ppermute(x, AXES, [(i, (i + distance) % group_size) for i in range(gr...  7.9 us
    pallas_call x1, Pallas kernels, per_device(): call(own_kernel, (jax.ShapeDtypeStruct((REQUESTS, heads, LATENT), bf16),...  3.7 us
    pallas_call x1, Pallas kernels, per_device(): call(send_kernel, (pltpu.HBM(message, bf16), jax.ShapeDtypeStruct((featur...  3.05 us
    pallas_call x1, Pallas kernels, per_device(): call(combine_kernel, (jax.ShapeDtypeStruct(moe_in.shape, bf16), jax.Shape...  2.28 us
  transfers between devices with their start and end apart: 3, of which 2 were waited for; matrix products, arithmetic and copies ran while one was open for 0% of the time, Pallas kernels for 18%

profile of v1, /device:TPU:0, one launch (start us, length us, event | category | flops | bytes accessed | tf_op | source)
XLA Modules:
  0.0 93.0 jit_solution(16758749634852103034)
XLA Ops:
  0.6 0.0 copy-start.5
  0.6 0.0 copy-start.6
  0.7 0.0 copy-start
  0.7 0.0 copy-start.1
  0.7 0.0 copy-start.2
  0.7 0.0 copy-start.3
  0.7 0.0 copy-start.4
  0.7 3.0 %shard_map.122 = (bf16[1024,896]{1,0:T(8,128)(2,1)}, bf16[576,128]{1,0:T(8,128)(2,1)S(1)}) custom-call(s32[384]{0:T(512)} %source_ref.5, s32[8,16]{1,0:T(8,128)} %bitcast.20, bf16[16,3584]{1,0:T(8,128)(2,1)} %x_hbm.1, bf16[3,576,128]{2,1,0:T(8,128)(2,1)} %bitcast.14), custom_call_target="tpu_custom_call" | custom-call | tf_op jit(solution)/shard_map/pallas_call | solution.py:253
  3.8 11.6 %all-to-all-start = ((bf16[128,8,896]{2,1,0:T(8,128)(2,1)}), bf16[128,8,896]{2,1,0:T(8,128)(2,1)}, u32[]{:S(2)}, u32[]{:S(2)}) async-start(bf16[128,8,896]{2,1,0:T(8,128)(2,1)} %bitcast.19), calls=%async_computation | async-start | bytes 3670016 | tf_op jit(solution)/shard_map/all_to_all | solution.py:243
  15.4 7.1 %collective-permute-start = (bf16[576,128]{1,0:T(8,128)(2,1)S(1)}, bf16[576,128]{1,0:T(8,128)(2,1)S(1)}, u32[]{:S(2)}, u32[]{:S(2)}) collective-permute-start(bf16[576,128]{1,0:T(8,128)(2,1)S(1)} %get-tuple-element.13), channel_id=1, source_target_pairs={{0,127},{1,0},{2,1},{3,2},{4,3},{5,4},{6,5},{7,6},{8,7},{9,8},{10,... | collective-permute-start | bytes 442376 | tf_op jit(solution)/shard_map/ppermute | solution.py:246
  22.4 0.0 copy-done.5
  22.4 0.1 copy.14.ids_ref
  22.5 0.0 copy-done.6
  22.5 0.1 copy.15.gates_ref
  22.6 0.0 copy-done
  22.6 0.0 copy-done.1
  22.6 0.0 copy-done.2
  22.6 0.0 copy-done.3
  22.6 0.0 copy-done.4
  22.6 3.7 %shard_map.124 = (bf16[3,128,512]{2,1,0:T(8,128)(2,1)}, bf16[192,1024]{1,0:T(8,128)(2,1)S(1)}) custom-call(s32[384]{0:T(512)S(1)} %copy-done.2, s32[384]{0:T(512)S(1)} %copy-done.3, s32[384]{0:T(512)S(1)} %copy-done.4, bf16[3,576,128]{2,1,0:T(8,128)(2,1)S(1)} %bitcast.15, bf16[1664,576]{1,0:T(8,128)(2,1)S(1)} %bitcast.10, s32[16,8]{1,0:T(8,128)S(1)} %copy.14.ids_ref, ...), custom_call_target="tpu_custom_call" | custom-call | tf_op jit(solution)/shard_map/pallas_call | solution.py:272
  26.3 12.7 %collective-permute-done.query_ref = bf16[576,128]{1,0:T(8,128)(2,1)S(1)} collective-permute-done((bf16[576,128]{1,0:T(8,128)(2,1)S(1)}, bf16[576,128]{1,0:T(8,128)(2,1)S(1)}, u32[]{:S(2)}, u32[]{:S(2)}) %collective-permute-start) | collective-permute-done | bytes 147488 | tf_op jit(solution)/shard_map/ppermute | solution.py:246
  39.0 1.7 %shard_map.123 = bf16[128,512]{1,0:T(8,128)(2,1)S(1)} custom-call(s32[384]{0:T(512)S(1)} %copy-done.2, s32[384]{0:T(512)S(1)} %copy-done.3, s32[384]{0:T(512)S(1)} %copy-done.4, bf16[576,128]{1,0:T(8,128)(2,1)S(1)} %collective-permute-done.query_ref, bf16[1664,576]{1,0:T(8,128)(2,1)S(1)} %bitcast.11), custom_call_target="tpu_custom_call" | custom-call | tf_op jit(solution)/shard_map/pallas_call | solution.py:281
  40.7 1.5 %all-to-all-done = bf16[128,8,896]{2,1,0:T(8,128)(2,1)} async-done(((bf16[128,8,896]{2,1,0:T(8,128)(2,1)}), bf16[128,8,896]{2,1,0:T(8,128)(2,1)}, u32[]{:S(2)}, u32[]{:S(2)}) %all-to-all-start) | async-done | bytes 1835040 | tf_op jit(solution)/shard_map/all_to_all | solution.py:243
  42.2 0.8 collective-permute-start.1
  43.0 11.6 %shard_map.125 = bf16[1024,896]{1,0:T(8,128)(2,1)S(1)} custom-call(bf16[1024,896]{1,0:T(8,128)(2,1)} %bitcast.3.x_ref, bf16[3584,1024]{1,0:T(8,128)(2,1)} %bitcast.16, bf16[3584,1024]{1,0:T(8,128)(2,1)} %bitcast.17, bf16[1024,3584]{1,0:T(8,128)(2,1)} %bitcast.18), custom_call_target="tpu_custom_call" | custom-call | tf_op jit(solution)/shard_map/pallas_call | solution.py:286
  54.6 0.0 collective-permute-done.1.moved_hbm
  54.6 36.1 %all_to_all.10 = bf16[128,8,896]{2,1,0:T(8,128)(2,1)S(1)} all-to-all(bf16[128,8,896]{2,1,0:T(8,128)(2,1)S(1)} %bitcast.12), channel_id=1, replica_groups=mesh['dp'=64,'chip'=2] {'dp','chip'}, dimensions={0} | all-to-all | bytes 3670016 | tf_op jit(solution)/shard_map/all_to_all | solution.py:243
  90.7 2.3 %shard_map.126 = (bf16[16,3584]{1,0:T(8,128)(2,1)}, bf16[3,128,512]{2,1,0:T(8,128)(2,1)}) custom-call(s32[384]{0:T(512)S(1)} %copy-done.2, bf16[192,1024]{1,0:T(8,128)(2,1)S(1)} %get-tuple-element.16.gates_ref, bf16[1024,896]{1,0:T(8,128)(2,1)S(1)} %bitcast.13, ...), custom_call_target="tpu_custom_call", output_to_operand_aliasing={{1}: (4, {})} | custom-call | tf_op jit(solution)/shard_map/pallas_call | solution.py:304
Async XLA Ops:
  0.6 21.8 %copy-start.5 = (s32[16,8]{0,1:T(8,128)S(1)}, s32[16,8]{0,1:T(8,128)}, u32[]{:S(2)}) copy-start(s32[16,8]{0,1:T(8,128)} %param.12) | copy-start | bytes 1540
  0.6 21.9 %copy-start.6 = (f32[16,8]{0,1:T(8,128)S(1)}, f32[16,8]{0,1:T(8,128)}, u32[]{:S(2)}) copy-start(f32[16,8]{0,1:T(8,128)} %param.13) | copy-start | bytes 1540
  0.7 21.9 %copy-start = (bf16[26,64,576]{2,1,0:T(8,128)(2,1)S(1)}, bf16[26,64,576]{2,1,0:T(8,128)(2,1)}, u32[]{:S(2)}) copy-start(bf16[26,64,576]{2,1,0:T(8,128)(2,1)} %param.18) | copy-start | bytes 5750788
  0.7 21.9 %copy-start.1 = (bf16[3,128,576]{1,2,0:T(8,128)(2,1)S(1)}, bf16[3,128,576]{1,2,0:T(8,128)(2,1)}, u32[]{:S(2)}) copy-start(bf16[3,128,576]{1,2,0:T(8,128)(2,1)} %param.17) | copy-start | bytes 1327108
  0.7 21.9 %copy-start.2 = (s32[384]{0:T(512)S(1)}, s32[384]{0:T(512)}, u32[]{:S(2)}) copy-start(s32[384]{0:T(512)} %source_ref.5) | copy-start | bytes 4612
  0.7 21.9 %copy-start.3 = (s32[384]{0:T(512)S(1)}, s32[384]{0:T(512)}, u32[]{:S(2)}) copy-start(s32[384]{0:T(512)} %first_ref.3) | copy-start | bytes 4612
  0.7 21.9 %copy-start.4 = (s32[384]{0:T(512)S(1)}, s32[384]{0:T(512)}, u32[]{:S(2)}) copy-start(s32[384]{0:T(512)} %tokens_ref.3) | copy-start | bytes 4612
  3.8 38.4 %all-to-all-start = ((bf16[128,8,896]{2,1,0:T(8,128)(2,1)}), bf16[128,8,896]{2,1,0:T(8,128)(2,1)}, u32[]{:S(2)}, u32[]{:S(2)}) async-start(bf16[128,8,896]{2,1,0:T(8,128)(2,1)} %bitcast.19), calls=%async_computation | async-start | bytes 3670016 | tf_op jit(solution)/shard_map/all_to_all | solution.py:243
  15.4 23.6 %collective-permute-start = (bf16[576,128]{1,0:T(8,128)(2,1)S(1)}, bf16[576,128]{1,0:T(8,128)(2,1)S(1)}, u32[]{:S(2)}, u32[]{:S(2)}) collective-permute-start(bf16[576,128]{1,0:T(8,128)(2,1)S(1)} %get-tuple-element.13), channel_id=1, source_target_pairs={{0,127},{1,0},{2,1},{3,2},{4,3},{5,4},{6,5},{7,6},{8,7},{9,8},{10,... | collective-permute-start | bytes 442376 | tf_op jit(solution)/shard_map/ppermute | solution.py:246
  42.2 12.4 %collective-permute-start.1 = (bf16[128,512]{1,0:T(8,128)(2,1)S(1)}, bf16[128,512]{1,0:T(8,128)(2,1)S(1)}, u32[]{:S(2)}, u32[]{:S(2)}) collective-permute-start(bf16[128,512]{1,0:T(8,128)(2,1)S(1)} %shard_map.123), channel_id=1, source_target_pairs={{0,1},{1,2},{2,3},{3,4},{4,5},{5,6},{6,7},{7,8},{8,9},{9,10},{10,1... | collective-permute-start | bytes 393224 | tf_op jit(solution)/shard_map/ppermute | solution.py:246

commit v2 on v1

--- a/solution.py
+++ b/solution.py
@@ -124,10 +124,7 @@
     for third in range(3):
         head = rest.astype(jnp.bfloat16)
         rest = rest - head.astype(jnp.float32)
-        spread_head = jnp.where(hit, dot(head, spread), 0.0)
-        for p in range(PARTS):
-            at = (third * PARTS + p) * rows
-            out_ref[at : at + rows, :] = jnp.where(place % PARTS == p, spread_head, 0.0).astype(jnp.bfloat16)
+        out_ref[third * rows : (third + 1) * rows, :] = jnp.where(hit, dot(head, spread), 0.0).astype(jnp.bfloat16)
 
 
 def window(cache_ref, first):
@@ -152,7 +149,7 @@
     out_ref[...] = attend(query_ref[...], window(cache_ref, first_ref[n]), tokens_ref[n])
 
 
-def expert_kernel(x_ref, gate_hbm, up_hbm, down_hbm, out_ref, gate_ref, up_ref, down_ref, wide, flat, hidden, sems):
+def expert_kernel(x_ref, gate_hbm, up_hbm, down_hbm, out_hbm, gate_ref, up_ref, down_ref, out_ref, wide, flat, hidden, sems):
     messages, piece = x_ref.shape
     units = hidden.shape[1]
     place_count = SLOTS * PARTS
@@ -185,6 +182,7 @@
         gate_part = dot(flat[...], gate_ref[:, n : n + STEP])
         up_part = dot(flat[...], up_ref[:, n : n + STEP])
         hidden[:, n : n + STEP] = (gate_part / (1.0 + jnp.exp(-gate_part)) * up_part).astype(jnp.bfloat16)
+    sends = []
     for low, group in zip(lows, far):
         high = min(low + STEP, piece)
         for copy in group:
@@ -198,19 +196,43 @@
                     wide[c, pl.ds(s * PARTS + p, ranks, stride=place_count), :] = kept
         for c in range(low // LANES, high // LANES):
             out_ref[:, c * LANES : (c + 1) * LANES] = wide[c].astype(jnp.bfloat16)
-
-
-def combine_kernel(source_ref, gates_ref, returned_ref, moved_hbm, attn_hbm, out_ref, attn_out_hbm, sem):
+        columns = pl.ds(low, high - low)
+        sends.append(pltpu.make_async_copy(out_ref.at[:, columns], out_hbm.at[:, columns], sems.at[count + len(sends)]))
+        sends[-1].start()
+    for send in sends:
+        send.wait()
+
+
+def combine_kernel(source_hbm, gates_hbm, returned_hbm, moved_ref, attn_hbm, out_ref, attn_out_hbm, source_ref, gates_ref, returned_ref, sems):
     del attn_hbm
-    my_rank = lax.axis_index(AXES)
-    mine = moved_at(source_ref, my_rank, REQUESTS)
-    copy = pltpu.make_async_copy(moved_hbm, attn_out_hbm.at[mine], sem)
+    messages, piece = returned_ref.shape
+    steps = 4
+    step = messages // steps
+    gates_copy = pltpu.make_async_copy(gates_hbm, gates_ref, sems.at[0])
+    source_copy = pltpu.make_async_copy(source_hbm, source_ref, sems.at[1])
+    gates_copy.start()
+    arrivals = []
+    for n in range(steps):
+        at = pl.ds(n * step, step)
+        arrivals.append(pltpu.make_async_copy(returned_hbm.at[at], returned_ref.at[at], sems.at[3 + n]))
+        arrivals[-1].start()
+    source_copy.start()
+    rows = out_ref.shape[0]
+    source_copy.wait()
+    mine = moved_at(source_ref, lax.axis_index(AXES), REQUESTS)
+    copy = pltpu.make_async_copy(moved_ref, attn_out_hbm.at[mine], sems.at[2])
     copy.start()
-    rows = out_ref.shape[0]
-    piece = returned_ref.shape[1]
-    total = dot(gates_ref[...], returned_ref[...])
+    gates_copy.wait()
+    part = iota((3 * rows, step), 1) % PARTS
+    total = jnp.zeros((PARTS * 3 * rows, piece), jnp.float32)
+    for n, arrival in enumerate(arrivals):
+        at = slice(n * step, (n + 1) * step)
+        gates = gates_ref[:, at]
+        split = jnp.concatenate([jnp.where(part == p, gates, jnp.zeros_like(gates)) for p in range(PARTS)], axis=0)
+        arrival.wait()
+        total += dot(split, returned_ref[at, :])
     for p in range(PARTS):
-        thirds = [total[(third * PARTS + p) * rows : (third * PARTS + p + 1) * rows] for third in range(3)]
+        thirds = [total[(p * 3 + third) * rows : (p * 3 + third + 1) * rows] for third in range(3)]
         out_ref[:, p * piece : (p + 1) * piece] = (thirds[0] + thirds[1] + thirds[2]).astype(jnp.bfloat16)
     copy.wait()
 
@@ -250,6 +272,7 @@
 
     message = (messages, piece)
     query_cols = jnp.swapaxes(queries, 1, 2)
+    cache_rows = cache_pool.reshape(-1, features)
     outgoing, moved_query = call(
         send_kernel,
         (pltpu.HBM(message, bf16), jax.ShapeDtypeStruct((features, heads), bf16)),
@@ -267,13 +290,31 @@
     moved_query = to_rank(moved_query, -1)
     arrived = exchange(outgoing)
 
-    cache_rows = cache_pool.reshape(-1, features)
     plan = (req_source, req_first, req_tokens)
+    answered = call(
+        expert_kernel,
+        pltpu.HBM(message, bf16),
+        [VMEM] + [HBM] * 3,
+        HBM,
+        [
+            pltpu.VMEM(gate_weight.shape[1:], bf16),
+            pltpu.VMEM(up_weight.shape[1:], bf16),
+            pltpu.VMEM(down_weight.shape[1:], bf16),
+            pltpu.VMEM(message, bf16),
+            pltpu.VMEM((piece // LANES, messages, LANES), jnp.float32),
+            pltpu.VMEM((SLOTS * group_size, model_width), bf16),
+            pltpu.VMEM((SLOTS * group_size, units), bf16),
+            dma((2 * (units // STEP) + (PARTS + 1) * -(-piece // STEP),)),
+        ],
+        limit=44 * MIB,
+    )(arrived, *stay(gate_weight[0], up_weight[0], down_weight[0]))
+    answered, moved_query, query_cols, cache_rows = lax.optimization_barrier((answered, moved_query, query_cols, cache_rows))
+    returned = exchange(answered)
     attn_own, gates = call(
         own_kernel,
         (
             jax.ShapeDtypeStruct((REQUESTS, heads, LATENT), bf16),
-            jax.ShapeDtypeStruct((3 * PARTS * row_count, messages), bf16),
+            jax.ShapeDtypeStruct((3 * row_count, messages), bf16),
         ),
         [SMEM] * 3 + [VMEM] * 4,
         (VMEM,) * 2,
@@ -281,34 +322,20 @@
     moved_out = call(moved_kernel, jax.ShapeDtypeStruct((heads, LATENT), bf16), [SMEM] * 3 + [VMEM] * 2, VMEM)(
         *plan, moved_query, cache_rows
     )
-    arrived, moved_out, attn_own, gates = lax.optimization_barrier((arrived, moved_out, attn_own, gates))
     moved_out = to_rank(moved_out, 1)
-    answered = call(
-        expert_kernel,
-        jax.ShapeDtypeStruct(message, bf16),
-        [VMEM] + [HBM] * 3,
-        VMEM,
-        [
-            pltpu.VMEM(gate_weight.shape[1:], bf16),
-            pltpu.VMEM(up_weight.shape[1:], bf16),
-            pltpu.VMEM(down_weight.shape[1:], bf16),
-            pltpu.VMEM((piece // LANES, messages, LANES), jnp.float32),
-            pltpu.VMEM((SLOTS * group_size, model_width), bf16),
-            pltpu.VMEM((SLOTS * group_size, units), bf16),
-            dma((2 * (units // STEP) + PARTS * -(-piece // STEP),)),
-        ],
-        limit=44 * MIB,
-    )(arrived, *stay(gate_weight[0], up_weight[0], down_weight[0]))
-    answered, moved_out = lax.optimization_barrier((answered, moved_out))
-    returned = exchange(answered)
     moe_out, attn_latent = call(
         combine_kernel,
-        (jax.ShapeDtypeStruct(moe_in.shape, bf16), jax.ShapeDtypeStruct(attn_own.shape, bf16)),
-        [SMEM, VMEM, VMEM, HBM, HBM],
+        (jax.ShapeDtypeStruct(moe_in.shape, bf16), pltpu.HBM(attn_own.shape, bf16)),
+        [HBM] * 3 + [VMEM, HBM],
         (VMEM, HBM),
-        [dma],
+        [
+            pltpu.SMEM(req_source.shape, jnp.int32),
+            pltpu.VMEM(gates.shape, bf16),
+            pltpu.VMEM(message, bf16),
+            dma((7,)),
+        ],
         aliases={4: 1},
-    )(req_source, gates, returned, moved_out, attn_own)
+    )(*stay(req_source, gates, returned), moved_out, *stay(attn_own))
     return (moe_out, attn_latent)
 
 

time: 93.4 us -> 90.2 us (0.966)
  blocking collectives: 36.1 us -> 0 us
  waiting for transfers between devices: 14.2 us -> 41 us
  starting transfers between devices: 19.5 us -> 25.2 us
    all_to_all x1 -> x0, blocking collectives: 36.1 us -> none  [exchange(): lax.all_to_all(x, AXES, split_axis=0, concat_axis=0, tiled=True)]
    all_to_all x1 -> x2, waiting for transfers between devices: 1.51 us -> 20 us  [exchange(): lax.all_to_all(x, AXES, split_axis=0, concat_axis=0, tiled=True)]
    ppermute x2, waiting for transfers between devices: 12.7 us -> 20.9 us  [to_rank(): lax.ppermute(x, AXES, [(i, (i + distance) % group_size) for i in range(gr...]
    all_to_all x1 -> x2, starting transfers between devices: 11.6 us -> 17 us  [exchange(): lax.all_to_all(x, AXES, split_axis=0, concat_axis=0, tiled=True)]
  transfers between devices with their start and end apart: 3 -> 4, of which waited for: 2 -> 2; matrix products, arithmetic and copies ran while one was open for 0% -> 0% of each run, Pallas kernels for 18% -> 18%
where the time goes in v2:
time: 90.2 us; the launch traced here: 89.8 us
  waiting for transfers between devices  41 us (45%)
  starting transfers between devices  25.2 us (28%)
  Pallas kernels  22 us (24%)
    ppermute x2, waiting for transfers between devices, to_rank(): lax.ppermute(x, AXES, [(i, (i + distance) % group_size) for i in range(gr...  20.9 us
    all_to_all x2, waiting for transfers between devices, exchange(): lax.all_to_all(x, AXES, split_axis=0, concat_axis=0, tiled=True)  20 us
    all_to_all x2, starting transfers between devices, exchange(): lax.all_to_all(x, AXES, split_axis=0, concat_axis=0, tiled=True)  17 us
    pallas_call x1, Pallas kernels, per_device(): call(expert_kernel, pltpu.HBM(message, bf16), [VMEM] + [HBM] * 3, HBM, [p...  10.9 us
    ppermute x2, starting transfers between devices, to_rank(): lax.ppermute(x, AXES, [(i, (i + distance) % group_size) for i in range(gr...  8.23 us
    pallas_call x1, Pallas kernels, per_device(): call(own_kernel, (jax.ShapeDtypeStruct((REQUESTS, heads, LATENT), bf16),...  3.7 us
    pallas_call x1, Pallas kernels, per_device(): call(combine_kernel, (jax.ShapeDtypeStruct(moe_in.shape, bf16), pltpu.HBM...  2.91 us
    pallas_call x1, Pallas kernels, per_device(): call(send_kernel, (pltpu.HBM(message, bf16), jax.ShapeDtypeStruct((featur...  2.89 us
  transfers between devices with their start and end apart: 4, of which 2 were waited for; matrix products, arithmetic and copies ran while one was open for 0% of the time, Pallas kernels for 18%

profile of v2, /device:TPU:0, one launch (start us, length us, event | category | flops | bytes accessed | tf_op | source)
XLA Modules:
  0.0 89.8 jit_solution(17836908216142740304)
XLA Ops:
  0.6 2.9 %shard_map.122 = (bf16[1024,896]{1,0:T(8,128)(2,1)}, bf16[576,128]{1,0:T(8,128)(2,1)S(1)}) custom-call(s32[384]{0:T(512)} %source_hbm.3, s32[8,16]{1,0:T(8,128)} %bitcast.20, bf16[16,3584]{1,0:T(8,128)(2,1)} %x_hbm.1, bf16[3,576,128]{2,1,0:T(8,128)(2,1)} %bitcast.13), custom_call_target="tpu_custom_call" | custom-call | tf_op jit(solution)/shard_map/pallas_call | solution.py:276
  3.5 11.2 %all-to-all-start = ((bf16[128,8,896]{2,1,0:T(8,128)(2,1)}), bf16[128,8,896]{2,1,0:T(8,128)(2,1)S(1)}, u32[]{:S(2)}, u32[]{:S(2)}) async-start(bf16[128,8,896]{2,1,0:T(8,128)(2,1)} %bitcast.19), calls=%async_computation | async-start | bytes 3670016 | tf_op jit(solution)/shard_map/all_to_all | solution.py:265
  14.7 7.1 %collective-permute-start = (bf16[576,128]{1,0:T(8,128)(2,1)S(1)}, bf16[576,128]{1,0:T(8,128)(2,1)S(1)}, u32[]{:S(2)}, u32[]{:S(2)}) collective-permute-start(bf16[576,128]{1,0:T(8,128)(2,1)S(1)} %get-tuple-element.11), channel_id=1, source_target_pairs={{0,127},{1,0},{2,1},{3,2},{4,3},{5,4},{6,5},{7,6},{8,7},{9,8},{10,... | collective-permute-start | bytes 442376 | tf_op jit(solution)/shard_map/ppermute | solution.py:268
  21.8 20.0 %all-to-all-done = bf16[128,8,896]{2,1,0:T(8,128)(2,1)S(1)} async-done(((bf16[128,8,896]{2,1,0:T(8,128)(2,1)}), bf16[128,8,896]{2,1,0:T(8,128)(2,1)S(1)}, u32[]{:S(2)}, u32[]{:S(2)}) %all-to-all-start) | async-done | bytes 1835040 | tf_op jit(solution)/shard_map/all_to_all | solution.py:265
  41.9 10.9 %shard_map.123 = bf16[1024,896]{1,0:T(8,128)(2,1)} custom-call(bf16[1024,896]{1,0:T(8,128)(2,1)S(1)} %bitcast.12, bf16[3584,1024]{1,0:T(8,128)(2,1)} %bitcast.16, bf16[3584,1024]{1,0:T(8,128)(2,1)} %bitcast.17, bf16[1024,3584]{1,0:T(8,128)(2,1)} %bitcast.18), custom_call_target="tpu_custom_call" | custom-call | tf_op jit(solution)/shard_map/pallas_call | solution.py:294
  52.7 0.0 copy-start
  52.8 0.0 copy-start.3
  52.8 0.0 copy-start.4
  52.8 0.0 copy-start.5
  52.8 0.0 collective-permute-done.query_ref
  52.8 0.0 copy-start.6
  52.8 5.9 %all-to-all-start.1 = ((bf16[128,8,896]{2,1,0:T(8,128)(2,1)}), bf16[128,8,896]{2,1,0:T(8,128)(2,1)}, u32[]{:S(2)}, u32[]{:S(2)}) async-start(bf16[128,8,896]{2,1,0:T(8,128)(2,1)} %bitcast.15), calls=%async_computation.1 | async-start | bytes 3670016 | tf_op jit(solution)/shard_map/all_to_all | solution.py:265
  58.7 0.0 copy-done
  58.7 0.0 copy-done.3
  58.7 0.0 copy-done.4
  58.7 0.0 copy-done.5
  58.7 0.0 copy-start.7
  58.7 0.0 copy-start.1
  58.7 1.7 %shard_map.125 = bf16[128,512]{1,0:T(8,128)(2,1)S(1)} custom-call(s32[384]{0:T(512)S(1)} %copy-done.3, s32[384]{0:T(512)S(1)} %copy-done.4, s32[384]{0:T(512)S(1)} %copy-done.5, bf16[576,128]{1,0:T(8,128)(2,1)S(1)} %collective-permute-done.query_ref, bf16[1664,576]{1,0:T(8,128)(2,1)S(1)} %bitcast.10), custom_call_target="tpu_custom_call" | custom-call | tf_op jit(solution)/shard_map/pallas_call | solution.py:322
  60.4 1.1 %collective-permute-start.1 = (bf16[128,512]{1,0:T(8,128)(2,1)S(1)}, bf16[128,512]{1,0:T(8,128)(2,1)S(1)}, u32[]{:S(2)}, u32[]{:S(2)}) collective-permute-start(bf16[128,512]{1,0:T(8,128)(2,1)S(1)} %shard_map.125), channel_id=1, source_target_pairs={{0,1},{1,2},{2,3},{3,4},{4,5},{5,6},{6,7},{7,8},{8,9},{9,10},{10,1... | collective-permute-start | bytes 393224 | tf_op jit(solution)/shard_map/ppermute | solution.py:268
  61.5 0.0 copy-done.6
  61.5 0.1 copy.14.ids_ref
  61.6 0.0 copy-done.7
  61.6 0.1 copy.15.gates_ref
  61.7 0.0 copy-done.1
  61.7 3.7 %shard_map.124 = (bf16[3,128,512]{2,1,0:T(8,128)(2,1)}, bf16[48,1024]{1,0:T(8,128)(2,1)S(1)}) custom-call(s32[384]{0:T(512)S(1)} %copy-done.3, s32[384]{0:T(512)S(1)} %copy-done.4, s32[384]{0:T(512)S(1)} %copy-done.5, bf16[3,576,128]{2,1,0:T(8,128)(2,1)S(1)} %bitcast.14, bf16[1664,576]{1,0:T(8,128)(2,1)S(1)} %bitcast.11, s32[16,8]{1,0:T(8,128)S(1)} %copy.14.ids_ref, ...), custom_call_target="tpu_custom_call" | custom-call | tf_op jit(solution)/shard_map/pallas_call | solution.py:313
  65.4 0.0 copy-start.2
  65.4 0.6 copy-done.2
  66.0 20.9 %collective-permute-done.1.moved_ref = bf16[128,512]{1,0:T(8,128)(2,1)S(1)} collective-permute-done((bf16[128,512]{1,0:T(8,128)(2,1)S(1)}, bf16[128,512]{1,0:T(8,128)(2,1)S(1)}, u32[]{:S(2)}, u32[]{:S(2)}) %collective-permute-start.1) | collective-permute-done | bytes 131104 | tf_op jit(solution)/shard_map/ppermute | solution.py:268
  86.9 0.0 all-to-all-done.1
  86.9 2.9 %shard_map.126 = (bf16[16,3584]{1,0:T(8,128)(2,1)}, bf16[3,128,512]{2,1,0:T(8,128)(2,1)}) custom-call(s32[384]{0:T(512)} %source_hbm.3, bf16[48,1024]{1,0:T(8,128)(2,1)} %copy-done.2, bf16[1024,896]{1,0:T(8,128)(2,1)} %bitcast.9.returned_hbm, bf16[128,512]{1,0:T(8,128)(2,1)S(1)} %collective-permute-done.1.moved_ref, ...), custom_call_target="tpu_custom_call", output_to_operand_aliasing={{1}: (4, {})} | custom-call | tf_op jit(solution)/shard_map/pallas_call | solution.py:326
Async XLA Ops:
  3.5 38.3 %all-to-all-start = ((bf16[128,8,896]{2,1,0:T(8,128)(2,1)}), bf16[128,8,896]{2,1,0:T(8,128)(2,1)S(1)}, u32[]{:S(2)}, u32[]{:S(2)}) async-start(bf16[128,8,896]{2,1,0:T(8,128)(2,1)} %bitcast.19), calls=%async_computation | async-start | bytes 3670016 | tf_op jit(solution)/shard_map/all_to_all | solution.py:265
  14.7 38.1 %collective-permute-start = (bf16[576,128]{1,0:T(8,128)(2,1)S(1)}, bf16[576,128]{1,0:T(8,128)(2,1)S(1)}, u32[]{:S(2)}, u32[]{:S(2)}) collective-permute-start(bf16[576,128]{1,0:T(8,128)(2,1)S(1)} %get-tuple-element.11), channel_id=1, source_target_pairs={{0,127},{1,0},{2,1},{3,2},{4,3},{5,4},{6,5},{7,6},{8,7},{9,8},{10,... | collective-permute-start | bytes 442376 | tf_op jit(solution)/shard_map/ppermute | solution.py:268
  52.7 5.9 %copy-start = (bf16[26,64,576]{2,1,0:T(8,128)(2,1)S(1)}, bf16[26,64,576]{2,1,0:T(8,128)(2,1)}, u32[]{:S(2)}) copy-start(bf16[26,64,576]{2,1,0:T(8,128)(2,1)} %param.18) | copy-start | bytes 5750788
  52.8 5.9 %copy-start.3 = (s32[384]{0:T(512)S(1)}, s32[384]{0:T(512)}, u32[]{:S(2)}) copy-start(s32[384]{0:T(512)} %source_hbm.3) | copy-start | bytes 4612
  52.8 5.9 %copy-start.4 = (s32[384]{0:T(512)S(1)}, s32[384]{0:T(512)}, u32[]{:S(2)}) copy-start(s32[384]{0:T(512)} %first_ref.3) | copy-start | bytes 4612
  52.8 5.9 %copy-start.5 = (s32[384]{0:T(512)S(1)}, s32[384]{0:T(512)}, u32[]{:S(2)}) copy-start(s32[384]{0:T(512)} %tokens_ref.3) | copy-start | bytes 4612
  52.8 8.7 %copy-start.6 = (s32[16,8]{0,1:T(8,128)S(1)}, s32[16,8]{0,1:T(8,128)}, u32[]{:S(2)}) copy-start(s32[16,8]{0,1:T(8,128)} %param.12) | copy-start | bytes 1540
  52.8 34.1 %all-to-all-start.1 = ((bf16[128,8,896]{2,1,0:T(8,128)(2,1)}), bf16[128,8,896]{2,1,0:T(8,128)(2,1)}, u32[]{:S(2)}, u32[]{:S(2)}) async-start(bf16[128,8,896]{2,1,0:T(8,128)(2,1)} %bitcast.15), calls=%async_computation.1 | async-start | bytes 3670016 | tf_op jit(solution)/shard_map/all_to_all | solution.py:265
  58.7 2.9 %copy-start.7 = (f32[16,8]{0,1:T(8,128)S(1)}, f32[16,8]{0,1:T(8,128)}, u32[]{:S(2)}) copy-start(f32[16,8]{0,1:T(8,128)} %param.13) | copy-start | bytes 1540
  58.7 2.9 %copy-start.1 = (bf16[3,128,576]{1,2,0:T(8,128)(2,1)S(1)}, bf16[3,128,576]{1,2,0:T(8,128)(2,1)}, u32[]{:S(2)}) copy-start(bf16[3,128,576]{1,2,0:T(8,128)(2,1)} %param.17) | copy-start | bytes 1327108
  60.4 26.5 %collective-permute-start.1 = (bf16[128,512]{1,0:T(8,128)(2,1)S(1)}, bf16[128,512]{1,0:T(8,128)(2,1)S(1)}, u32[]{:S(2)}, u32[]{:S(2)}) collective-permute-start(bf16[128,512]{1,0:T(8,128)(2,1)S(1)} %shard_map.125), channel_id=1, source_target_pairs={{0,1},{1,2},{2,3},{3,4},{4,5},{5,6},{6,7},{7,8},{8,9},{9,10},{10,1... | collective-permute-start | bytes 393224 | tf_op jit(solution)/shard_map/ppermute | solution.py:268
  65.4 0.6 copy-start.2

commit v3 on v2

--- a/solution.py
+++ b/solution.py
@@ -9,7 +9,7 @@
 
 LATENT = 512
 MAX_BLOCKS = 12
-POOL = 26
+BLOCK_ROWS = 64
 REQUESTS = 3
 SLOTS = 2
 PARTS = 4
@@ -127,26 +127,41 @@
         out_ref[third * rows : (third + 1) * rows, :] = jnp.where(hit, dot(head, spread), 0.0).astype(jnp.bfloat16)
 
 
-def window(cache_ref, first):
-    block_rows = cache_ref.shape[0] // POOL
-    start = pl.multiple_of(first * block_rows, block_rows)
-    return cache_ref[pl.ds(start, MAX_BLOCKS * block_rows), :]
-
-
-def own_kernel(source_ref, first_ref, tokens_ref, queries_ref, cache_ref, ids_ref, gates_ref, attn_ref, spread_ref):
-    spread_gates(ids_ref, gates_ref, spread_ref)
+def fetch_request(queries_hbm, cache_hbm, first, query_ref, rows_ref, sems):
+    start = pl.multiple_of(first * BLOCK_ROWS, BLOCK_ROWS)
+    copies = [
+        pltpu.make_async_copy(queries_hbm, query_ref, sems.at[0]),
+        pltpu.make_async_copy(cache_hbm.at[pl.ds(start, rows_ref.shape[0])], rows_ref, sems.at[1]),
+    ]
+    for copy in copies:
+        copy.start()
+    return copies
+
+
+def own_kernel(
+    source_ref, first_ref, tokens_ref, queries_hbm, cache_hbm, ids_ref, gates_ref, attn_ref, spread_ref, query_ref, rows_ref, sems
+):
     my_rank = lax.axis_index(AXES)
     mine = moved_at(source_ref, my_rank, REQUESTS)
-    for r in (jnp.where(mine == 0, 1, 0), jnp.where(mine == 2, 1, 2)):
-        n = my_rank * REQUESTS + r
-        attn_ref[r] = attend(queries_ref[r], window(cache_ref, first_ref[n]), tokens_ref[n])
+    own = (jnp.where(mine == 0, 1, 0), jnp.where(mine == 2, 1, 2))
+    copies = []
+    for i, r in enumerate(own):
+        first = first_ref[my_rank * REQUESTS + r]
+        copies.append(fetch_request(queries_hbm.at[r], cache_hbm, first, query_ref.at[i], rows_ref.at[i], sems.at[i]))
+    spread_gates(ids_ref, gates_ref, spread_ref)
+    for i, r in enumerate(own):
+        for copy in copies[i]:
+            copy.wait()
+        attn_ref[r] = attend(query_ref[i], rows_ref[i], tokens_ref[my_rank * REQUESTS + r])
     attn_ref[mine] = jnp.zeros(attn_ref.shape[1:], attn_ref.dtype)
 
 
-def moved_kernel(source_ref, first_ref, tokens_ref, query_ref, cache_ref, out_ref):
+def moved_kernel(source_ref, first_ref, tokens_ref, query_hbm, cache_hbm, out_ref, query_ref, rows_ref, sems):
     next_rank = lax.rem(lax.axis_index(AXES) + 1, source_ref.shape[0] // REQUESTS)
     n = next_rank * REQUESTS + moved_at(source_ref, next_rank, REQUESTS)
-    out_ref[...] = attend(query_ref[...], window(cache_ref, first_ref[n]), tokens_ref[n])
+    for copy in fetch_request(query_hbm, cache_hbm, first_ref[n], query_ref, rows_ref, sems):
+        copy.wait()
+    out_ref[...] = attend(query_ref[...], rows_ref[...], tokens_ref[n])
 
 
 def expert_kernel(x_ref, gate_hbm, up_hbm, down_hbm, out_hbm, gate_ref, up_ref, down_ref, out_ref, wide, flat, hidden, sems):
@@ -203,34 +218,17 @@
         send.wait()
 
 
-def combine_kernel(source_hbm, gates_hbm, returned_hbm, moved_ref, attn_hbm, out_ref, attn_out_hbm, source_ref, gates_ref, returned_ref, sems):
+def combine_kernel(source_ref, gates_ref, returned_ref, moved_ref, attn_hbm, out_ref, attn_out_hbm, sem):
     del attn_hbm
-    messages, piece = returned_ref.shape
-    steps = 4
-    step = messages // steps
-    gates_copy = pltpu.make_async_copy(gates_hbm, gates_ref, sems.at[0])
-    source_copy = pltpu.make_async_copy(source_hbm, source_ref, sems.at[1])
-    gates_copy.start()
-    arrivals = []
-    for n in range(steps):
-        at = pl.ds(n * step, step)
-        arrivals.append(pltpu.make_async_copy(returned_hbm.at[at], returned_ref.at[at], sems.at[3 + n]))
-        arrivals[-1].start()
-    source_copy.start()
+    mine = moved_at(source_ref, lax.axis_index(AXES), REQUESTS)
+    copy = pltpu.make_async_copy(moved_ref, attn_out_hbm.at[mine], sem)
+    copy.start()
     rows = out_ref.shape[0]
-    source_copy.wait()
-    mine = moved_at(source_ref, lax.axis_index(AXES), REQUESTS)
-    copy = pltpu.make_async_copy(moved_ref, attn_out_hbm.at[mine], sems.at[2])
-    copy.start()
-    gates_copy.wait()
-    part = iota((3 * rows, step), 1) % PARTS
-    total = jnp.zeros((PARTS * 3 * rows, piece), jnp.float32)
-    for n, arrival in enumerate(arrivals):
-        at = slice(n * step, (n + 1) * step)
-        gates = gates_ref[:, at]
-        split = jnp.concatenate([jnp.where(part == p, gates, jnp.zeros_like(gates)) for p in range(PARTS)], axis=0)
-        arrival.wait()
-        total += dot(split, returned_ref[at, :])
+    piece = returned_ref.shape[1]
+    gates = gates_ref[...]
+    part = iota(gates.shape, 1) % PARTS
+    split = jnp.concatenate([jnp.where(part == p, gates, jnp.zeros_like(gates)) for p in range(PARTS)], axis=0)
+    total = dot(split, returned_ref[...])
     for p in range(PARTS):
         thirds = [total[(p * 3 + third) * rows : (p * 3 + third + 1) * rows] for third in range(3)]
         out_ref[:, p * piece : (p + 1) * piece] = (thirds[0] + thirds[1] + thirds[2]).astype(jnp.bfloat16)
@@ -316,26 +314,34 @@
             jax.ShapeDtypeStruct((REQUESTS, heads, LATENT), bf16),
             jax.ShapeDtypeStruct((3 * row_count, messages), bf16),
         ),
-        [SMEM] * 3 + [VMEM] * 4,
+        [SMEM] * 3 + [HBM] * 2 + [VMEM] * 2,
         (VMEM,) * 2,
-    )(*plan, query_cols, cache_rows, expert_ids, expert_gates)
-    moved_out = call(moved_kernel, jax.ShapeDtypeStruct((heads, LATENT), bf16), [SMEM] * 3 + [VMEM] * 2, VMEM)(
-        *plan, moved_query, cache_rows
-    )
+        [
+            pltpu.VMEM((REQUESTS - 1, features, heads), bf16),
+            pltpu.VMEM((REQUESTS - 1, MAX_BLOCKS * BLOCK_ROWS, features), bf16),
+            dma((REQUESTS - 1, 2)),
+        ],
+    )(*plan, *stay(query_cols, cache_rows), expert_ids, expert_gates)
+    moved_out = call(
+        moved_kernel,
+        jax.ShapeDtypeStruct((heads, LATENT), bf16),
+        [SMEM] * 3 + [HBM] * 2,
+        VMEM,
+        [
+            pltpu.VMEM((features, heads), bf16),
+            pltpu.VMEM((MAX_BLOCKS * BLOCK_ROWS, features), bf16),
+            dma((2,)),
+        ],
+    )(*plan, moved_query, *stay(cache_rows))
     moved_out = to_rank(moved_out, 1)
     moe_out, attn_latent = call(
         combine_kernel,
         (jax.ShapeDtypeStruct(moe_in.shape, bf16), pltpu.HBM(attn_own.shape, bf16)),
-        [HBM] * 3 + [VMEM, HBM],
+        [SMEM] + [VMEM] * 3 + [HBM],
         (VMEM, HBM),
-        [
-            pltpu.SMEM(req_source.shape, jnp.int32),
-            pltpu.VMEM(gates.shape, bf16),
-            pltpu.VMEM(message, bf16),
-            dma((7,)),
-        ],
+        [dma],
         aliases={4: 1},
-    )(*stay(req_source, gates, returned), moved_out, *stay(attn_own))
+    )(req_source, gates, returned, moved_out, *stay(attn_own))
     return (moe_out, attn_latent)
 
 

time: 90.2 us -> 88.9 us (0.986)
  Pallas kernels: 22 us -> 24.1 us
  waiting for transfers between devices: 41 us -> 39.4 us
  starting transfers between devices: 25.2 us -> 24.1 us
    ppermute x2, waiting for transfers between devices: 20.9 us -> 19.3 us  [to_rank(): lax.ppermute(x, AXES, [(i, (i + distance) % group_size) for i in range(gr...]
    pallas_call x1, Pallas kernels: 1.66 us -> 3.1 us  [per_device(): call(moved_kernel, jax.ShapeDtypeStruct((heads, LATENT), bf16), [SMEM] *...]
    pallas_call x1, Pallas kernels: 3.7 us -> 4.9 us  [per_device(): call(own_kernel, (jax.ShapeDtypeStruct((REQUESTS, heads, LATENT), bf16),...]
    all_to_all x2, starting transfers between devices: 17 us -> 15.8 us  [exchange(): lax.all_to_all(x, AXES, split_axis=0, concat_axis=0, tiled=True)]
  transfers between devices with their start and end apart: 4 -> 4, of which waited for: 2 -> 2; matrix products, arithmetic and copies ran while one was open for 0% -> 0% of each run, Pallas kernels for 18% -> 21%
where the time goes in v3:
time: 88.9 us; the launch traced here: 88.6 us
  waiting for transfers between devices  39.4 us (44%)
  Pallas kernels  24.1 us (27%)
  starting transfers between devices  24.1 us (27%)
    all_to_all x2, waiting for transfers between devices, exchange(): lax.all_to_all(x, AXES, split_axis=0, concat_axis=0, tiled=True)  20 us
    ppermute x2, waiting for transfers between devices, to_rank(): lax.ppermute(x, AXES, [(i, (i + distance) % group_size) for i in range(gr...  19.3 us
    all_to_all x2, starting transfers between devices, exchange(): lax.all_to_all(x, AXES, split_axis=0, concat_axis=0, tiled=True)  15.8 us
    pallas_call x1, Pallas kernels, per_device(): call(expert_kernel, pltpu.HBM(message, bf16), [VMEM] + [HBM] * 3, HBM, [p...  10.9 us
    ppermute x2, starting transfers between devices, to_rank(): lax.ppermute(x, AXES, [(i, (i + distance) % group_size) for i in range(gr...  8.29 us
    pallas_call x1, Pallas kernels, per_device(): call(own_kernel, (jax.ShapeDtypeStruct((REQUESTS, heads, LATENT), bf16),...  4.9 us
    pallas_call x1, Pallas kernels, per_device(): call(moved_kernel, jax.ShapeDtypeStruct((heads, LATENT), bf16), [SMEM] *...  3.1 us
    pallas_call x1, Pallas kernels, per_device(): call(send_kernel, (pltpu.HBM(message, bf16), jax.ShapeDtypeStruct((featur...  2.87 us
  transfers between devices with their start and end apart: 4, of which 2 were waited for; matrix products, arithmetic and copies ran while one was open for 0% of the time, Pallas kernels for 21%

profile of v3, /device:TPU:0, one launch (start us, length us, event | category | flops | bytes accessed | tf_op | source)
XLA Modules:
  0.0 88.6 jit_solution(13693325064534563757)
XLA Ops:
  0.6 2.9 %shard_map.122 = (bf16[1024,896]{1,0:T(8,128)(2,1)}, bf16[576,128]{1,0:T(8,128)(2,1)S(1)}) custom-call(s32[384]{0:T(512)} %source_ref.5, s32[8,16]{1,0:T(8,128)} %bitcast.21, bf16[16,3584]{1,0:T(8,128)(2,1)} %x_hbm.1, bf16[3,576,128]{2,1,0:T(8,128)(2,1)} %bitcast.19), custom_call_target="tpu_custom_call" | custom-call | tf_op jit(solution)/shard_map/pallas_call | solution.py:274
  3.5 11.2 %all-to-all-start = ((bf16[128,8,896]{2,1,0:T(8,128)(2,1)}), bf16[128,8,896]{2,1,0:T(8,128)(2,1)S(1)}, u32[]{:S(2)}, u32[]{:S(2)}) async-start(bf16[128,8,896]{2,1,0:T(8,128)(2,1)} %bitcast.18), calls=%async_computation | async-start | bytes 3670016 | tf_op jit(solution)/shard_map/all_to_all | solution.py:263
  14.7 7.1 %collective-permute-start = (bf16[576,128]{1,0:T(8,128)(2,1)S(1)}, bf16[576,128]{1,0:T(8,128)(2,1)S(1)}, u32[]{:S(2)}, u32[]{:S(2)}) collective-permute-start(bf16[576,128]{1,0:T(8,128)(2,1)S(1)} %get-tuple-element.11), channel_id=1, source_target_pairs={{0,127},{1,0},{2,1},{3,2},{4,3},{5,4},{6,5},{7,6},{8,7},{9,8},{10,... | collective-permute-start | bytes 442376 | tf_op jit(solution)/shard_map/ppermute | solution.py:266
  21.8 20.0 %all-to-all-done = bf16[128,8,896]{2,1,0:T(8,128)(2,1)S(1)} async-done(((bf16[128,8,896]{2,1,0:T(8,128)(2,1)}), bf16[128,8,896]{2,1,0:T(8,128)(2,1)S(1)}, u32[]{:S(2)}, u32[]{:S(2)}) %all-to-all-start) | async-done | bytes 1835040 | tf_op jit(solution)/shard_map/all_to_all | solution.py:263
  41.8 10.9 %shard_map.123 = bf16[1024,896]{1,0:T(8,128)(2,1)} custom-call(bf16[1024,896]{1,0:T(8,128)(2,1)S(1)} %bitcast.10, bf16[3584,1024]{1,0:T(8,128)(2,1)} %bitcast.15, bf16[3584,1024]{1,0:T(8,128)(2,1)} %bitcast.16, bf16[1024,3584]{1,0:T(8,128)(2,1)} %bitcast.17), custom_call_target="tpu_custom_call" | custom-call | tf_op jit(solution)/shard_map/pallas_call | solution.py:292
  52.7 0.0 copy-start
  52.7 0.0 copy-start.1
  52.7 0.0 copy-start.2
  52.7 0.0 collective-permute-done.query_hbm
  52.8 0.0 copy-start.3
  52.8 4.7 %all-to-all-start.1 = ((bf16[128,8,896]{2,1,0:T(8,128)(2,1)}), bf16[128,8,896]{2,1,0:T(8,128)(2,1)S(1)}, u32[]{:S(2)}, u32[]{:S(2)}) async-start(bf16[128,8,896]{2,1,0:T(8,128)(2,1)} %bitcast.14), calls=%async_computation.1 | async-start | bytes 3670016 | tf_op jit(solution)/shard_map/all_to_all | solution.py:263
  57.5 0.0 copy-done
  57.5 0.0 copy-done.1
  57.5 0.0 copy-done.2
  57.5 0.0 copy-start.4
  57.5 3.1 %shard_map.125 = bf16[128,512]{1,0:T(8,128)(2,1)S(1)} custom-call(s32[384]{0:T(512)S(1)} %copy-done, s32[384]{0:T(512)S(1)} %copy-done.1, s32[384]{0:T(512)S(1)} %copy-done.2, bf16[576,128]{1,0:T(8,128)(2,1)S(1)} %collective-permute-done.query_hbm, bf16[1664,576]{1,0:T(8,128)(2,1)} %bitcast.12), custom_call_target="tpu_custom_call" | custom-call | tf_op jit(solution)/shard_map/pallas_call | solution.py:325
  60.6 1.2 %collective-permute-start.1 = (bf16[128,512]{1,0:T(8,128)(2,1)S(1)}, bf16[128,512]{1,0:T(8,128)(2,1)S(1)}, u32[]{:S(2)}, u32[]{:S(2)}) collective-permute-start(bf16[128,512]{1,0:T(8,128)(2,1)S(1)} %shard_map.125), channel_id=1, source_target_pairs={{0,1},{1,2},{2,3},{3,4},{4,5},{5,6},{6,7},{7,8},{8,9},{9,10},{10,1... | collective-permute-start | bytes 393224 | tf_op jit(solution)/shard_map/ppermute | solution.py:266
  61.8 0.0 copy-done.3
  61.8 0.1 copy.14.ids_ref
  61.9 0.0 copy-done.4
  61.9 0.1 copy.15.gates_ref
  61.9 4.9 %shard_map.124 = (bf16[3,128,512]{2,1,0:T(8,128)(2,1)}, bf16[48,1024]{1,0:T(8,128)(2,1)S(1)}) custom-call(s32[384]{0:T(512)S(1)} %copy-done, s32[384]{0:T(512)S(1)} %copy-done.1, s32[384]{0:T(512)S(1)} %copy-done.2, bf16[3,576,128]{2,1,0:T(8,128)(2,1)} %bitcast.20, bf16[1664,576]{1,0:T(8,128)(2,1)} %bitcast.13, s32[16,8]{1,0:T(8,128)S(1)} %copy.14.ids_ref, ...), custom_call_target="tpu_custom_call" | custom-call | tf_op jit(solution)/shard_map/pallas_call | solution.py:311
  66.8 19.3 %collective-permute-done.1.moved_ref = bf16[128,512]{1,0:T(8,128)(2,1)S(1)} collective-permute-done((bf16[128,512]{1,0:T(8,128)(2,1)S(1)}, bf16[128,512]{1,0:T(8,128)(2,1)S(1)}, u32[]{:S(2)}, u32[]{:S(2)}) %collective-permute-start.1) | collective-permute-done | bytes 131104 | tf_op jit(solution)/shard_map/ppermute | solution.py:266
  86.2 0.0 all-to-all-done.1
  86.2 2.4 %shard_map.126 = (bf16[16,3584]{1,0:T(8,128)(2,1)}, bf16[3,128,512]{2,1,0:T(8,128)(2,1)}) custom-call(s32[384]{0:T(512)S(1)} %copy-done, bf16[48,1024]{1,0:T(8,128)(2,1)S(1)} %get-tuple-element.14.gates_ref, bf16[1024,896]{1,0:T(8,128)(2,1)S(1)} %bitcast.11, bf16[128,512]{1,0:T(8,128)(2,1)S(1)} %collective-permute-done.1.moved_ref, ...), custom_call_target="tpu_custom_call", output_to_operand_aliasing={{1}: (4, {})} | custom-call | tf_op jit(solution)/shard_map/pallas_call | solution.py:337
Async XLA Ops:
  3.5 38.3 %all-to-all-start = ((bf16[128,8,896]{2,1,0:T(8,128)(2,1)}), bf16[128,8,896]{2,1,0:T(8,128)(2,1)S(1)}, u32[]{:S(2)}, u32[]{:S(2)}) async-start(bf16[128,8,896]{2,1,0:T(8,128)(2,1)} %bitcast.18), calls=%async_computation | async-start | bytes 3670016 | tf_op jit(solution)/shard_map/all_to_all | solution.py:263
  14.7 38.1 %collective-permute-start = (bf16[576,128]{1,0:T(8,128)(2,1)S(1)}, bf16[576,128]{1,0:T(8,128)(2,1)S(1)}, u32[]{:S(2)}, u32[]{:S(2)}) collective-permute-start(bf16[576,128]{1,0:T(8,128)(2,1)S(1)} %get-tuple-element.11), channel_id=1, source_target_pairs={{0,127},{1,0},{2,1},{3,2},{4,3},{5,4},{6,5},{7,6},{8,7},{9,8},{10,... | collective-permute-start | bytes 442376 | tf_op jit(solution)/shard_map/ppermute | solution.py:266
  52.7 4.8 %copy-start = (s32[384]{0:T(512)S(1)}, s32[384]{0:T(512)}, u32[]{:S(2)}) copy-start(s32[384]{0:T(512)} %source_ref.5) | copy-start | bytes 4612
  52.7 4.8 %copy-start.1 = (s32[384]{0:T(512)S(1)}, s32[384]{0:T(512)}, u32[]{:S(2)}) copy-start(s32[384]{0:T(512)} %first_ref.3) | copy-start | bytes 4612
  52.7 4.8 %copy-start.2 = (s32[384]{0:T(512)S(1)}, s32[384]{0:T(512)}, u32[]{:S(2)}) copy-start(s32[384]{0:T(512)} %tokens_ref.3) | copy-start | bytes 4612
  52.8 9.0 %copy-start.3 = (s32[16,8]{0,1:T(8,128)S(1)}, s32[16,8]{0,1:T(8,128)}, u32[]{:S(2)}) copy-start(s32[16,8]{0,1:T(8,128)} %param.12) | copy-start | bytes 1540
  52.8 33.4 %all-to-all-start.1 = ((bf16[128,8,896]{2,1,0:T(8,128)(2,1)}), bf16[128,8,896]{2,1,0:T(8,128)(2,1)S(1)}, u32[]{:S(2)}, u32[]{:S(2)}) async-start(bf16[128,8,896]{2,1,0:T(8,128)(2,1)} %bitcast.14), calls=%async_computation.1 | async-start | bytes 3670016 | tf_op jit(solution)/shard_map/all_to_all | solution.py:263
  57.5 4.4 %copy-start.4 = (f32[16,8]{0,1:T(8,128)S(1)}, f32[16,8]{0,1:T(8,128)}, u32[]{:S(2)}) copy-start(f32[16,8]{0,1:T(8,128)} %param.13) | copy-start | bytes 1540
  60.6 25.6 %collective-permute-start.1 = (bf16[128,512]{1,0:T(8,128)(2,1)S(1)}, bf16[128,512]{1,0:T(8,128)(2,1)S(1)}, u32[]{:S(2)}, u32[]{:S(2)}) collective-permute-start(bf16[128,512]{1,0:T(8,128)(2,1)S(1)} %shard_map.125), channel_id=1, source_target_pairs={{0,1},{1,2},{2,3},{3,4},{4,5},{5,6},{6,7},{7,8},{8,9},{9,10},{10,1... | collective-permute-start | bytes 393224 | tf_op jit(solution)/shard_map/ppermute | solution.py:266

commit v4 on v3

--- a/solution.py
+++ b/solution.py
@@ -16,6 +16,7 @@
 LANES = 128
 MIB = 1 << 20
 STEP = 256
+AHEAD = pl.CostEstimate(flops=20_000_000_000, transcendentals=0, bytes_accessed=40_000_000)
 
 score_scale = 1.0 / math.sqrt(192.0)
 
@@ -25,7 +26,7 @@
 AXES = ("dp", "chip")
 
 
-def call(kernel, out_shape, in_specs, out_specs, scratch=(), limit=24 * MIB, aliases={}):
+def call(kernel, out_shape, in_specs, out_specs, scratch=(), limit=24 * MIB, aliases={}, cost=None):
     return pl.pallas_call(
         kernel,
         out_shape=out_shape,
@@ -33,6 +34,7 @@
         out_specs=out_specs,
         scratch_shapes=scratch,
         input_output_aliases=aliases,
+        cost_estimate=cost,
         compiler_params=pltpu.CompilerParams(vmem_limit_bytes=limit),
     )
 
@@ -53,7 +55,7 @@
     return lax.broadcasted_iota(jnp.int32, shape, dim)
 
 
-def send_kernel(source_hbm, ids_hbm, x_hbm, queries_hbm, out_hbm, query_ref, source_ref, ids_ref, x_ref, queries_ref, out_ref, sems):
+def send_kernel(source_hbm, ids_hbm, x_hbm, queries_hbm, out_ref, query_ref, source_ref, ids_ref, x_ref, queries_ref, sems):
     pairs = ((ids_hbm, ids_ref), (x_hbm, x_ref), (source_hbm, source_ref), (queries_hbm, queries_ref))
     fetches = [pltpu.make_async_copy(here, there, sems.at[i]) for i, (here, there) in enumerate(pairs)]
     for fetch in fetches:
@@ -78,20 +80,15 @@
     pieces = jnp.concatenate([x_ref[:, p * piece : (p + 1) * piece] for p in range(PARTS)], axis=0)
     steps = 4
     step = messages // steps
-    sends = []
     for n in range(steps):
         at = n * step
         spread = ((iota((step, ranks), 0) + at) // place_count == iota((step, ranks), 1)).astype(jnp.bfloat16)
         place = iota((step, columns), 0) % place_count
         hit = (dot(spread, slot) == (place // PARTS).astype(jnp.float32)) & (place % PARTS == iota((step, columns), 1) // rows)
         out_ref[at : at + step, :] = dot(hit.astype(jnp.bfloat16), pieces).astype(jnp.bfloat16)
-        sends.append(pltpu.make_async_copy(out_ref.at[pl.ds(at, step)], out_hbm.at[pl.ds(at, step)], sems.at[4 + n]))
-        sends[-1].start()
     fetches[2].wait()
     fetches[3].wait()
     query_ref[...] = queries_ref[moved_at(source_ref, lax.axis_index(AXES), REQUESTS)]
-    for send in sends:
-        send.wait()
 
 
 def attend(query_cols, cache_rows, length):
@@ -164,25 +161,13 @@
     out_ref[...] = attend(query_ref[...], rows_ref[...], tokens_ref[n])
 
 
-def expert_kernel(x_ref, gate_hbm, up_hbm, down_hbm, out_hbm, gate_ref, up_ref, down_ref, out_ref, wide, flat, hidden, sems):
+def expert_kernel(x_ref, gate_ref, up_ref, down_ref, out_hbm, out_ref, wide, flat, hidden, sems):
     messages, piece = x_ref.shape
     units = hidden.shape[1]
     place_count = SLOTS * PARTS
     ranks = messages // place_count
     strips = piece // LANES
-    count = 0
-
-    def fetch(here, there, at, width):
-        nonlocal count
-        columns = pl.ds(at, width)
-        copy = pltpu.make_async_copy(here.at[:, columns], there.at[:, columns], sems.at[count])
-        copy.start()
-        count += 1
-        return copy
-
-    near = [(fetch(gate_hbm, gate_ref, n, STEP), fetch(up_hbm, up_ref, n, STEP)) for n in range(0, units, STEP)]
     lows = range(0, piece, STEP)
-    far = [[fetch(down_hbm, down_ref, p * piece + low, min(STEP, piece - low)) for p in range(PARTS)] for low in lows]
     for c in range(strips):
         wide[c] = x_ref[:, c * LANES : (c + 1) * LANES].astype(jnp.float32)
     for place in range(place_count):
@@ -191,17 +176,13 @@
             at = p * piece + c * LANES
             taken = wide[c, pl.ds(place, ranks, stride=place_count), :]
             flat[s * ranks : (s + 1) * ranks, at : at + LANES] = taken.astype(jnp.bfloat16)
-    for n, group in zip(range(0, units, STEP), near):
-        for copy in group:
-            copy.wait()
+    for n in range(0, units, STEP):
         gate_part = dot(flat[...], gate_ref[:, n : n + STEP])
         up_part = dot(flat[...], up_ref[:, n : n + STEP])
         hidden[:, n : n + STEP] = (gate_part / (1.0 + jnp.exp(-gate_part)) * up_part).astype(jnp.bfloat16)
     sends = []
-    for low, group in zip(lows, far):
+    for low in lows:
         high = min(low + STEP, piece)
-        for copy in group:
-            copy.wait()
         for p in range(PARTS):
             result = dot(hidden[...], down_ref[:, p * piece + low : p * piece + high])
             for s in range(SLOTS):
@@ -212,7 +193,7 @@
         for c in range(low // LANES, high // LANES):
             out_ref[:, c * LANES : (c + 1) * LANES] = wide[c].astype(jnp.bfloat16)
         columns = pl.ds(low, high - low)
-        sends.append(pltpu.make_async_copy(out_ref.at[:, columns], out_hbm.at[:, columns], sems.at[count + len(sends)]))
+        sends.append(pltpu.make_async_copy(out_ref.at[:, columns], out_hbm.at[:, columns], sems.at[len(sends)]))
         sends[-1].start()
     for send in sends:
         send.wait()
@@ -273,39 +254,37 @@
     cache_rows = cache_pool.reshape(-1, features)
     outgoing, moved_query = call(
         send_kernel,
-        (pltpu.HBM(message, bf16), jax.ShapeDtypeStruct((features, heads), bf16)),
+        (jax.ShapeDtypeStruct(message, bf16), jax.ShapeDtypeStruct((features, heads), bf16)),
         [HBM] * 4,
-        (HBM, VMEM),
+        (VMEM, VMEM),
         [
             pltpu.SMEM(req_source.shape, jnp.int32),
             pltpu.VMEM(expert_ids.shape[::-1], jnp.int32),
             pltpu.VMEM(moe_in.shape, bf16),
             pltpu.VMEM(query_cols.shape, bf16),
-            pltpu.VMEM(message, bf16),
-            dma((8,)),
+            dma((4,)),
         ],
+        cost=AHEAD,
     )(*stay(req_source, expert_ids.T, moe_in, query_cols))
+    arrived = exchange(outgoing)
+    arrived, moved_query = lax.optimization_barrier((arrived, moved_query))
     moved_query = to_rank(moved_query, -1)
-    arrived = exchange(outgoing)
 
     plan = (req_source, req_first, req_tokens)
     answered = call(
         expert_kernel,
         pltpu.HBM(message, bf16),
-        [VMEM] + [HBM] * 3,
+        [VMEM] * 4,
         HBM,
         [
-            pltpu.VMEM(gate_weight.shape[1:], bf16),
-            pltpu.VMEM(up_weight.shape[1:], bf16),
-            pltpu.VMEM(down_weight.shape[1:], bf16),
             pltpu.VMEM(message, bf16),
             pltpu.VMEM((piece // LANES, messages, LANES), jnp.float32),
             pltpu.VMEM((SLOTS * group_size, model_width), bf16),
             pltpu.VMEM((SLOTS * group_size, units), bf16),
-            dma((2 * (units // STEP) + (PARTS + 1) * -(-piece // STEP),)),
+            dma((-(-piece // STEP),)),
         ],
-        limit=44 * MIB,
-    )(arrived, *stay(gate_weight[0], up_weight[0], down_weight[0]))
+        limit=16 * MIB,
+    )(arrived, *[pltpu.with_memory_space_constraint(w[0], pltpu.VMEM) for w in (gate_weight, up_weight, down_weight)])
     answered, moved_query, query_cols, cache_rows = lax.optimization_barrier((answered, moved_query, query_cols, cache_rows))
     returned = exchange(answered)
     attn_own, gates = call(

time: 88.9 us -> 87.2 us (0.981)
  blocking collectives: 0 us -> 38.1 us
  waiting for transfers between devices: 39.4 us -> 19.3 us
  starting transfers between devices: 24.1 us -> 7.74 us
  Pallas kernels: 24.1 us -> 20.7 us
    all_to_all x0 -> x1, blocking collectives: none -> 38.1 us  [exchange(): lax.all_to_all(x, AXES, split_axis=0, concat_axis=0, tiled=True)]
    all_to_all x2 -> x1, waiting for transfers between devices: 20 us -> 0.01 us  [exchange(): lax.all_to_all(x, AXES, split_axis=0, concat_axis=0, tiled=True)]
    all_to_all x2 -> x1, starting transfers between devices: 15.8 us -> 4.84 us  [exchange(): lax.all_to_all(x, AXES, split_axis=0, concat_axis=0, tiled=True)]
    ppermute x2, starting transfers between devices: 8.29 us -> 2.9 us  [to_rank(): lax.ppermute(x, AXES, [(i, (i + distance) % group_size) for i in range(gr...]
    pallas_call x2, Pallas kernels: 13.7 us -> 10.3 us  [the longest x1 8.01 us: per_device(): call(expert_kernel, pltpu.HBM(message, bf16), [VMEM] * 4, HBM, [pltpu.VME...]
  transfers between devices with their start and end apart: 4 -> 3, of which waited for: 2 -> 1; matrix products, arithmetic and copies ran while one was open for 0% -> 0% of each run, Pallas kernels for 21% -> 18%
where the time goes in v4:
time: 87.2 us; the launch traced here: 86.9 us
  blocking collectives  38.1 us (44%)
  Pallas kernels  20.7 us (24%)
  waiting for transfers between devices  19.3 us (22%)
  starting transfers between devices  7.74 us (9%)
    all_to_all x1, blocking collectives, exchange(): lax.all_to_all(x, AXES, split_axis=0, concat_axis=0, tiled=True)  38.1 us
    ppermute x2, waiting for transfers between devices, to_rank(): lax.ppermute(x, AXES, [(i, (i + distance) % group_size) for i in range(gr...  19.3 us
    pallas_call x1, Pallas kernels, per_device(): call(expert_kernel, pltpu.HBM(message, bf16), [VMEM] * 4, HBM, [pltpu.VME...  8.01 us
    pallas_call x1, Pallas kernels, per_device(): call(own_kernel, (jax.ShapeDtypeStruct((REQUESTS, heads, LATENT), bf16),...  4.9 us
    all_to_all x1, starting transfers between devices, exchange(): lax.all_to_all(x, AXES, split_axis=0, concat_axis=0, tiled=True)  4.84 us
    pallas_call x1, Pallas kernels, per_device(): call(moved_kernel, jax.ShapeDtypeStruct((heads, LATENT), bf16), [SMEM] *...  3.1 us
    ppermute x2, starting transfers between devices, to_rank(): lax.ppermute(x, AXES, [(i, (i + distance) % group_size) for i in range(gr...  2.9 us
    pallas_call x1, Pallas kernels, per_device(): call(combine_kernel, (jax.ShapeDtypeStruct(moe_in.shape, bf16), pltpu.HBM...  2.4 us
  transfers between devices with their start and end apart: 3, of which 1 were waited for; matrix products, arithmetic and copies ran while one was open for 0% of the time, Pallas kernels for 18%

profile of v4, /device:TPU:0, one launch (start us, length us, event | category | flops | bytes accessed | tf_op | source)
XLA Modules:
  0.0 86.9 jit_solution(12532315559481294811)
XLA Ops:
  0.6 0.0 slice-start
  0.6 0.0 slice-start.2
  0.7 0.0 slice-start.4
  0.7 0.0 slice-start.1
  0.7 0.0 slice-start.3
  0.7 0.0 slice-start.5
  0.7 2.3 %shard_map.122 = (bf16[1024,896]{1,0:T(8,128)(2,1)S(1)}, bf16[576,128]{1,0:T(8,128)(2,1)S(1)}) custom-call(s32[384]{0:T(512)} %source_ref.5, s32[8,16]{1,0:T(8,128)} %bitcast.27, bf16[16,3584]{1,0:T(8,128)(2,1)} %x_hbm.1, bf16[3,576,128]{2,1,0:T(8,128)(2,1)} %bitcast.25), custom_call_target="tpu_custom_call" | custom-call | flops 20000000000 | bytes 40000000 | tf_op jit(solution)/shard_map/pallas_call | solution.py:255
  3.0 38.1 %all_to_all.10 = bf16[128,8,896]{2,1,0:T(8,128)(2,1)S(1)} all-to-all(bf16[128,8,896]{2,1,0:T(8,128)(2,1)S(1)} %bitcast.21), channel_id=1, replica_groups=mesh['dp'=64,'chip'=2] {'dp','chip'}, dimensions={0} | all-to-all | bytes 3670016 | tf_op jit(solution)/shard_map/all_to_all | solution.py:244
  41.1 1.7 %collective-permute-start = (bf16[576,128]{1,0:T(8,128)(2,1)S(1)}, bf16[576,128]{1,0:T(8,128)(2,1)S(1)}, u32[]{:S(2)}, u32[]{:S(2)}) collective-permute-start(bf16[576,128]{1,0:T(8,128)(2,1)S(1)} %get-tuple-element.15), channel_id=1, source_target_pairs={{0,127},{1,0},{2,1},{3,2},{4,3},{5,4},{6,5},{7,6},{8,7},{9,8},{10,... | collective-permute-start | bytes 442376 | tf_op jit(solution)/shard_map/ppermute | solution.py:247
  42.8 0.0 slice-done
  42.8 0.0 slice-done.2
  42.8 0.0 slice-done.4
  42.8 0.0 slice-done.1
  42.8 0.0 slice-done.3
  42.8 0.0 slice-done.5
  42.9 8.0 %shard_map.123 = bf16[1024,896]{1,0:T(8,128)(2,1)} custom-call(bf16[1024,896]{1,0:T(8,128)(2,1)S(1)} %bitcast.10, bf16[3584,1024]{1,0:T(8,128)(2,1)S(1)} %bitcast.14, bf16[3584,1024]{1,0:T(8,128)(2,1)S(1)} %bitcast.17, bf16[1024,3584]{1,0:T(8,128)(2,1)S(1)} %bitcast.20), custom_call_target="tpu_custom_call" | custom-call | tf_op jit(solution)/shard_map/pallas_call | solution.py:274
  50.9 0.0 copy-start
  50.9 0.0 copy-start.1
  50.9 0.0 copy-start.2
  50.9 0.0 collective-permute-done.query_hbm
  50.9 0.0 copy-start.3
  51.0 4.8 %all-to-all-start.1 = ((bf16[128,8,896]{2,1,0:T(8,128)(2,1)}), bf16[128,8,896]{2,1,0:T(8,128)(2,1)S(1)}, u32[]{:S(2)}, u32[]{:S(2)}) async-start(bf16[128,8,896]{2,1,0:T(8,128)(2,1)} %bitcast.24), calls=%async_computation.1 | async-start | bytes 3670016 | tf_op jit(solution)/shard_map/all_to_all | solution.py:244
  55.8 0.0 copy-done
  55.8 0.0 copy-done.1
  55.8 0.0 copy-done.2
  55.8 0.0 copy-start.4
  55.8 3.1 %shard_map.125 = bf16[128,512]{1,0:T(8,128)(2,1)S(1)} custom-call(s32[384]{0:T(512)S(1)} %copy-done, s32[384]{0:T(512)S(1)} %copy-done.1, s32[384]{0:T(512)S(1)} %copy-done.2, bf16[576,128]{1,0:T(8,128)(2,1)S(1)} %collective-permute-done.query_hbm, bf16[1664,576]{1,0:T(8,128)(2,1)} %bitcast.22), custom_call_target="tpu_custom_call" | custom-call | tf_op jit(solution)/shard_map/pallas_call | solution.py:304
  59.0 1.2 %collective-permute-start.1 = (bf16[128,512]{1,0:T(8,128)(2,1)S(1)}, bf16[128,512]{1,0:T(8,128)(2,1)S(1)}, u32[]{:S(2)}, u32[]{:S(2)}) collective-permute-start(bf16[128,512]{1,0:T(8,128)(2,1)S(1)} %shard_map.125), channel_id=1, source_target_pairs={{0,1},{1,2},{2,3},{3,4},{4,5},{5,6},{6,7},{7,8},{8,9},{9,10},{10,1... | collective-permute-start | bytes 393224 | tf_op jit(solution)/shard_map/ppermute | solution.py:247
  60.1 0.0 copy-done.3
  60.1 0.1 copy.14.ids_ref
  60.2 0.0 copy-done.4
  60.2 0.1 copy.15.gates_ref
  60.3 4.9 %shard_map.124 = (bf16[3,128,512]{2,1,0:T(8,128)(2,1)}, bf16[48,1024]{1,0:T(8,128)(2,1)S(1)}) custom-call(s32[384]{0:T(512)S(1)} %copy-done, s32[384]{0:T(512)S(1)} %copy-done.1, s32[384]{0:T(512)S(1)} %copy-done.2, bf16[3,576,128]{2,1,0:T(8,128)(2,1)} %bitcast.26, bf16[1664,576]{1,0:T(8,128)(2,1)} %bitcast.23, s32[16,8]{1,0:T(8,128)S(1)} %copy.14.ids_ref, ...), custom_call_target="tpu_custom_call" | custom-call | tf_op jit(solution)/shard_map/pallas_call | solution.py:290
  65.2 19.3 %collective-permute-done.1.moved_ref = bf16[128,512]{1,0:T(8,128)(2,1)S(1)} collective-permute-done((bf16[128,512]{1,0:T(8,128)(2,1)S(1)}, bf16[128,512]{1,0:T(8,128)(2,1)S(1)}, u32[]{:S(2)}, u32[]{:S(2)}) %collective-permute-start.1) | collective-permute-done | bytes 131104 | tf_op jit(solution)/shard_map/ppermute | solution.py:247
  84.5 0.0 all-to-all-done.1
  84.5 2.4 %shard_map.126 = (bf16[16,3584]{1,0:T(8,128)(2,1)}, bf16[3,128,512]{2,1,0:T(8,128)(2,1)}) custom-call(s32[384]{0:T(512)S(1)} %copy-done, bf16[48,1024]{1,0:T(8,128)(2,1)S(1)} %get-tuple-element.18.gates_ref, bf16[1024,896]{1,0:T(8,128)(2,1)S(1)} %bitcast.11, bf16[128,512]{1,0:T(8,128)(2,1)S(1)} %collective-permute-done.1.moved_ref, ...), custom_call_target="tpu_custom_call", output_to_operand_aliasing={{1}: (4, {})} | custom-call | tf_op jit(solution)/shard_map/pallas_call | solution.py:316
  (3 shorter events, 0.0 us)
Async XLA Ops:
  0.6 42.2 %slice-start = ((s8[7340032]{0:T(1024)(128)(4,1)}), s8[4194304]{0:T(1024)(128)(4,1)S(1)}, s32[]{:S(2)}) async-start(s8[7340032]{0:T(1024)(128)(4,1)} %bitcast.12), calls=%async_computation.2 | async-start | bytes 8388608
  0.6 42.2 %slice-start.2 = ((s8[7340032]{0:T(1024)(128)(4,1)}), s8[4194304]{0:T(1024)(128)(4,1)S(1)}, s32[]{:S(2)}) async-start(s8[7340032]{0:T(1024)(128)(4,1)} %bitcast.15), calls=%async_computation.4 | async-start | bytes 8388608
  0.7 42.2 %slice-start.4 = ((s8[7340032]{0:T(1024)(128)(4,1)}), s8[4194304]{0:T(1024)(128)(4,1)S(1)}, s32[]{:S(2)}) async-start(s8[7340032]{0:T(1024)(128)(4,1)} %bitcast.18), calls=%async_computation.6 | async-start | bytes 8388608
  0.7 42.2 %slice-start.1 = ((s8[7340032]{0:T(1024)(128)(4,1)}), s8[3145728]{0:T(1024)(128)(4,1)S(1)}, s32[]{:S(2)}) async-start(s8[7340032]{0:T(1024)(128)(4,1)} %bitcast.12), calls=%async_computation.3 | async-start | bytes 6291456
  0.7 42.2 %slice-start.3 = ((s8[7340032]{0:T(1024)(128)(4,1)}), s8[3145728]{0:T(1024)(128)(4,1)S(1)}, s32[]{:S(2)}) async-start(s8[7340032]{0:T(1024)(128)(4,1)} %bitcast.15), calls=%async_computation.5 | async-start | bytes 6291456
  0.7 42.2 %slice-start.5 = ((s8[7340032]{0:T(1024)(128)(4,1)}), s8[3145728]{0:T(1024)(128)(4,1)S(1)}, s32[]{:S(2)}) async-start(s8[7340032]{0:T(1024)(128)(4,1)} %bitcast.18), calls=%async_computation.7 | async-start | bytes 6291456
  41.1 9.9 %collective-permute-start = (bf16[576,128]{1,0:T(8,128)(2,1)S(1)}, bf16[576,128]{1,0:T(8,128)(2,1)S(1)}, u32[]{:S(2)}, u32[]{:S(2)}) collective-permute-start(bf16[576,128]{1,0:T(8,128)(2,1)S(1)} %get-tuple-element.15), channel_id=1, source_target_pairs={{0,127},{1,0},{2,1},{3,2},{4,3},{5,4},{6,5},{7,6},{8,7},{9,8},{10,... | collective-permute-start | bytes 442376 | tf_op jit(solution)/shard_map/ppermute | solution.py:247
  50.9 4.9 %copy-start = (s32[384]{0:T(512)S(1)}, s32[384]{0:T(512)}, u32[]{:S(2)}) copy-start(s32[384]{0:T(512)} %source_ref.5) | copy-start | bytes 4612
  50.9 4.9 %copy-start.1 = (s32[384]{0:T(512)S(1)}, s32[384]{0:T(512)}, u32[]{:S(2)}) copy-start(s32[384]{0:T(512)} %first_ref.3) | copy-start | bytes 4612
  50.9 4.9 %copy-start.2 = (s32[384]{0:T(512)S(1)}, s32[384]{0:T(512)}, u32[]{:S(2)}) copy-start(s32[384]{0:T(512)} %tokens_ref.3) | copy-start | bytes 4612
  50.9 9.2 %copy-start.3 = (s32[16,8]{0,1:T(8,128)S(1)}, s32[16,8]{0,1:T(8,128)}, u32[]{:S(2)}) copy-start(s32[16,8]{0,1:T(8,128)} %param.12) | copy-start | bytes 1540
  51.0 33.6 %all-to-all-start.1 = ((bf16[128,8,896]{2,1,0:T(8,128)(2,1)}), bf16[128,8,896]{2,1,0:T(8,128)(2,1)S(1)}, u32[]{:S(2)}, u32[]{:S(2)}) async-start(bf16[128,8,896]{2,1,0:T(8,128)(2,1)} %bitcast.24), calls=%async_computation.1 | async-start | bytes 3670016 | tf_op jit(solution)/shard_map/all_to_all | solution.py:244
  55.8 4.4 %copy-start.4 = (f32[16,8]{0,1:T(8,128)S(1)}, f32[16,8]{0,1:T(8,128)}, u32[]{:S(2)}) copy-start(f32[16,8]{0,1:T(8,128)} %param.13) | copy-start | bytes 1540
  59.0 25.5 %collective-permute-start.1 = (bf16[128,512]{1,0:T(8,128)(2,1)S(1)}, bf16[128,512]{1,0:T(8,128)(2,1)S(1)}, u32[]{:S(2)}, u32[]{:S(2)}) collective-permute-start(bf16[128,512]{1,0:T(8,128)(2,1)S(1)} %shard_map.125), channel_id=1, source_target_pairs={{0,1},{1,2},{2,3},{3,4},{4,5},{5,6},{6,7},{7,8},{8,9},{9,10},{10,1... | collective-permute-start | bytes 393224 | tf_op jit(solution)/shard_map/ppermute | solution.py:247

commit v5 on v4

--- a/solution.py
+++ b/solution.py
@@ -69,6 +69,10 @@
     before = (iota(shape, 0) // rows == iota(shape, 1) // rows) & (iota(shape, 0) < iota(shape, 1))
     before = before.astype(jnp.bfloat16)
     expert = iota((ranks, columns), 0)
+    spread = (iota((messages, ranks), 0) // place_count == iota((messages, ranks), 1)).astype(jnp.bfloat16)
+    place = iota((messages, columns), 0) % place_count
+    same_part = place % PARTS == iota((messages, columns), 1) // rows
+    wanted = jnp.where(same_part, (place // PARTS).astype(jnp.float32), float(SLOTS))
     fetches[0].wait()
     ids = jnp.concatenate([ids_ref[...]] * PARTS, axis=1)
     named = jnp.zeros((ranks, columns), jnp.float32)
@@ -76,16 +80,10 @@
         named += (ids[k : k + 1, :] == expert).astype(jnp.float32)
     named = named.astype(jnp.bfloat16)
     slot = jnp.where(named > 0, dot(named, before), -1.0).astype(jnp.bfloat16)
+    hit = (dot(spread, slot) == wanted).astype(jnp.bfloat16)
     fetches[1].wait()
     pieces = jnp.concatenate([x_ref[:, p * piece : (p + 1) * piece] for p in range(PARTS)], axis=0)
-    steps = 4
-    step = messages // steps
-    for n in range(steps):
-        at = n * step
-        spread = ((iota((step, ranks), 0) + at) // place_count == iota((step, ranks), 1)).astype(jnp.bfloat16)
-        place = iota((step, columns), 0) % place_count
-        hit = (dot(spread, slot) == (place // PARTS).astype(jnp.float32)) & (place % PARTS == iota((step, columns), 1) // rows)
-        out_ref[at : at + step, :] = dot(hit.astype(jnp.bfloat16), pieces).astype(jnp.bfloat16)
+    out_ref[...] = dot(hit, pieces).astype(jnp.bfloat16)
     fetches[2].wait()
     fetches[3].wait()
     query_ref[...] = queries_ref[moved_at(source_ref, lax.axis_index(AXES), REQUESTS)]
@@ -199,11 +197,10 @@
         send.wait()
 
 
-def combine_kernel(source_ref, gates_ref, returned_ref, moved_ref, attn_hbm, out_ref, attn_out_hbm, sem):
+def combine_kernel(source_hbm, gates_ref, returned_ref, moved_ref, attn_hbm, out_hbm, attn_out_hbm, source_ref, out_ref, sems):
     del attn_hbm
-    mine = moved_at(source_ref, lax.axis_index(AXES), REQUESTS)
-    copy = pltpu.make_async_copy(moved_ref, attn_out_hbm.at[mine], sem)
-    copy.start()
+    fetch = pltpu.make_async_copy(source_hbm, source_ref, sems.at[0])
+    fetch.start()
     rows = out_ref.shape[0]
     piece = returned_ref.shape[1]
     gates = gates_ref[...]
@@ -213,7 +210,14 @@
     for p in range(PARTS):
         thirds = [total[(p * 3 + third) * rows : (p * 3 + third + 1) * rows] for third in range(3)]
         out_ref[:, p * piece : (p + 1) * piece] = (thirds[0] + thirds[1] + thirds[2]).astype(jnp.bfloat16)
-    copy.wait()
+    out_copy = pltpu.make_async_copy(out_ref, out_hbm, sems.at[1])
+    out_copy.start()
+    fetch.wait()
+    mine = moved_at(source_ref, lax.axis_index(AXES), REQUESTS)
+    attn_copy = pltpu.make_async_copy(moved_ref, attn_out_hbm.at[mine], sems.at[2])
+    attn_copy.start()
+    out_copy.wait()
+    attn_copy.wait()
 
 
 def per_device(
@@ -315,12 +319,12 @@
     moved_out = to_rank(moved_out, 1)
     moe_out, attn_latent = call(
         combine_kernel,
-        (jax.ShapeDtypeStruct(moe_in.shape, bf16), pltpu.HBM(attn_own.shape, bf16)),
-        [SMEM] + [VMEM] * 3 + [HBM],
-        (VMEM, HBM),
-        [dma],
+        (pltpu.HBM(moe_in.shape, bf16), pltpu.HBM(attn_own.shape, bf16)),
+        [HBM] + [VMEM] * 3 + [HBM],
+        (HBM, HBM),
+        [pltpu.SMEM(req_source.shape, jnp.int32), pltpu.VMEM(moe_in.shape, bf16), dma((3,))],
         aliases={4: 1},
-    )(req_source, gates, returned, moved_out, *stay(attn_own))
+    )(*stay(req_source), gates, returned, moved_out, *stay(attn_own))
     return (moe_out, attn_latent)
 
 

time: 87.2 us -> 86.5 us (level)
  transfers between devices with their start and end apart: 3 -> 3, of which waited for: 1 -> 1; matrix products, arithmetic and copies ran while one was open for 0% -> 0% of each run, Pallas kernels for 18% -> 19%
where the time goes in v5:
time: 86.5 us; the launch traced here: 86.3 us
  blocking collectives  38.1 us (44%)
  Pallas kernels  20 us (23%)
  waiting for transfers between devices  19.3 us (22%)
  starting transfers between devices  7.72 us (9%)
    all_to_all x1, blocking collectives, exchange(): lax.all_to_all(x, AXES, split_axis=0, concat_axis=0, tiled=True)  38.1 us
    ppermute x2, waiting for transfers between devices, to_rank(): lax.ppermute(x, AXES, [(i, (i + distance) % group_size) for i in range(gr...  19.3 us
    pallas_call x1, Pallas kernels, per_device(): call(expert_kernel, pltpu.HBM(message, bf16), [VMEM] * 4, HBM, [pltpu.VME...  8.02 us
    pallas_call x1, Pallas kernels, per_device(): call(own_kernel, (jax.ShapeDtypeStruct((REQUESTS, heads, LATENT), bf16),...  4.9 us
    all_to_all x1, starting transfers between devices, exchange(): lax.all_to_all(x, AXES, split_axis=0, concat_axis=0, tiled=True)  4.82 us
    pallas_call x1, Pallas kernels, per_device(): call(moved_kernel, jax.ShapeDtypeStruct((heads, LATENT), bf16), [SMEM] *...  3.1 us
    ppermute x2, starting transfers between devices, to_rank(): lax.ppermute(x, AXES, [(i, (i + distance) % group_size) for i in range(gr...  2.9 us
    pallas_call x1, Pallas kernels, per_device(): call(send_kernel, (jax.ShapeDtypeStruct(message, bf16), jax.ShapeDtypeStr...  2.11 us
  transfers between devices with their start and end apart: 3, of which 1 were waited for; matrix products, arithmetic and copies ran while one was open for 0% of the time, Pallas kernels for 19%

profile of v5, /device:TPU:0, one launch (start us, length us, event | category | flops | bytes accessed | tf_op | source)
XLA Modules:
  0.0 86.3 jit_solution(5824165619027801912)
XLA Ops:
  0.6 0.0 slice-start
  0.6 0.0 slice-start.2
  0.7 0.0 slice-start.4
  0.7 0.0 slice-start.1
  0.7 0.0 slice-start.3
  0.7 0.0 slice-start.5
  0.7 2.1 %shard_map.122 = (bf16[1024,896]{1,0:T(8,128)(2,1)S(1)}, bf16[576,128]{1,0:T(8,128)(2,1)S(1)}) custom-call(s32[384]{0:T(512)} %source_hbm.3, s32[8,16]{1,0:T(8,128)} %bitcast.27, bf16[16,3584]{1,0:T(8,128)(2,1)} %x_hbm.1, bf16[3,576,128]{2,1,0:T(8,128)(2,1)} %bitcast.25), custom_call_target="tpu_custom_call" | custom-call | flops 20000000000 | bytes 40000000 | tf_op jit(solution)/shard_map/pallas_call | solution.py:259
  2.8 38.1 %all_to_all.10 = bf16[128,8,896]{2,1,0:T(8,128)(2,1)S(1)} all-to-all(bf16[128,8,896]{2,1,0:T(8,128)(2,1)S(1)} %bitcast.21), channel_id=1, replica_groups=mesh['dp'=64,'chip'=2] {'dp','chip'}, dimensions={0} | all-to-all | bytes 3670016 | tf_op jit(solution)/shard_map/all_to_all | solution.py:248
  40.9 1.7 %collective-permute-start = (bf16[576,128]{1,0:T(8,128)(2,1)S(1)}, bf16[576,128]{1,0:T(8,128)(2,1)S(1)}, u32[]{:S(2)}, u32[]{:S(2)}) collective-permute-start(bf16[576,128]{1,0:T(8,128)(2,1)S(1)} %get-tuple-element.15), channel_id=1, source_target_pairs={{0,127},{1,0},{2,1},{3,2},{4,3},{5,4},{6,5},{7,6},{8,7},{9,8},{10,... | collective-permute-start | bytes 442376 | tf_op jit(solution)/shard_map/ppermute | solution.py:251
  42.7 0.0 slice-done
  42.7 0.0 slice-done.2
  42.7 0.0 slice-done.4
  42.7 0.0 slice-done.1
  42.7 0.0 slice-done.3
  42.7 0.0 slice-done.5
  42.7 8.0 %shard_map.123 = bf16[1024,896]{1,0:T(8,128)(2,1)} custom-call(bf16[1024,896]{1,0:T(8,128)(2,1)S(1)} %bitcast.10, bf16[3584,1024]{1,0:T(8,128)(2,1)S(1)} %bitcast.14, bf16[3584,1024]{1,0:T(8,128)(2,1)S(1)} %bitcast.17, bf16[1024,3584]{1,0:T(8,128)(2,1)S(1)} %bitcast.20), custom_call_target="tpu_custom_call" | custom-call | tf_op jit(solution)/shard_map/pallas_call | solution.py:278
  50.8 0.0 copy-start
  50.8 0.0 copy-start.1
  50.8 0.0 copy-start.2
  50.8 0.0 collective-permute-done.query_hbm
  50.8 0.0 copy-start.3
  50.8 4.8 %all-to-all-start.1 = ((bf16[128,8,896]{2,1,0:T(8,128)(2,1)}), bf16[128,8,896]{2,1,0:T(8,128)(2,1)S(1)}, u32[]{:S(2)}, u32[]{:S(2)}) async-start(bf16[128,8,896]{2,1,0:T(8,128)(2,1)} %bitcast.24), calls=%async_computation.1 | async-start | bytes 3670016 | tf_op jit(solution)/shard_map/all_to_all | solution.py:248
  55.6 0.0 copy-done
  55.7 0.0 copy-done.1
  55.7 0.0 copy-done.2
  55.7 0.0 copy-start.4
  55.7 3.1 %shard_map.125 = bf16[128,512]{1,0:T(8,128)(2,1)S(1)} custom-call(s32[384]{0:T(512)S(1)} %copy-done, s32[384]{0:T(512)S(1)} %copy-done.1, s32[384]{0:T(512)S(1)} %copy-done.2, bf16[576,128]{1,0:T(8,128)(2,1)S(1)} %collective-permute-done.query_hbm, bf16[1664,576]{1,0:T(8,128)(2,1)} %bitcast.22), custom_call_target="tpu_custom_call" | custom-call | tf_op jit(solution)/shard_map/pallas_call | solution.py:308
  58.8 1.2 %collective-permute-start.1 = (bf16[128,512]{1,0:T(8,128)(2,1)S(1)}, bf16[128,512]{1,0:T(8,128)(2,1)S(1)}, u32[]{:S(2)}, u32[]{:S(2)}) collective-permute-start(bf16[128,512]{1,0:T(8,128)(2,1)S(1)} %shard_map.125), channel_id=1, source_target_pairs={{0,1},{1,2},{2,3},{3,4},{4,5},{5,6},{6,7},{7,8},{8,9},{9,10},{10,1... | collective-permute-start | bytes 393224 | tf_op jit(solution)/shard_map/ppermute | solution.py:251
  60.0 0.0 copy-done.3
  60.0 0.1 copy.14.ids_ref
  60.0 0.0 copy-done.4
  60.0 0.1 copy.15.gates_ref
  60.1 4.9 %shard_map.124 = (bf16[3,128,512]{2,1,0:T(8,128)(2,1)}, bf16[48,1024]{1,0:T(8,128)(2,1)S(1)}) custom-call(s32[384]{0:T(512)S(1)} %copy-done, s32[384]{0:T(512)S(1)} %copy-done.1, s32[384]{0:T(512)S(1)} %copy-done.2, bf16[3,576,128]{2,1,0:T(8,128)(2,1)} %bitcast.26, bf16[1664,576]{1,0:T(8,128)(2,1)} %bitcast.23, s32[16,8]{1,0:T(8,128)S(1)} %copy.14.ids_ref, ...), custom_call_target="tpu_custom_call" | custom-call | tf_op jit(solution)/shard_map/pallas_call | solution.py:294
  65.0 19.3 %collective-permute-done.1.moved_ref = bf16[128,512]{1,0:T(8,128)(2,1)S(1)} collective-permute-done((bf16[128,512]{1,0:T(8,128)(2,1)S(1)}, bf16[128,512]{1,0:T(8,128)(2,1)S(1)}, u32[]{:S(2)}, u32[]{:S(2)}) %collective-permute-start.1) | collective-permute-done | bytes 131104 | tf_op jit(solution)/shard_map/ppermute | solution.py:251
  84.4 0.0 all-to-all-done.1
  84.4 1.9 %shard_map.126 = (bf16[16,3584]{1,0:T(8,128)(2,1)}, bf16[3,128,512]{2,1,0:T(8,128)(2,1)}) custom-call(s32[384]{0:T(512)} %source_hbm.3, bf16[48,1024]{1,0:T(8,128)(2,1)S(1)} %get-tuple-element.18.gates_ref, bf16[1024,896]{1,0:T(8,128)(2,1)S(1)} %bitcast.11, bf16[128,512]{1,0:T(8,128)(2,1)S(1)} %collective-permute-done.1.moved_ref, ...), custom_call_target="tpu_custom_call", output_to_operand_aliasing={{1}: (4, {})} | custom-call | tf_op jit(solution)/shard_map/pallas_call | solution.py:320
  (3 shorter events, 0.0 us)
Async XLA Ops:
  0.6 42.0 %slice-start = ((s8[7340032]{0:T(1024)(128)(4,1)}), s8[4194304]{0:T(1024)(128)(4,1)S(1)}, s32[]{:S(2)}) async-start(s8[7340032]{0:T(1024)(128)(4,1)} %bitcast.12), calls=%async_computation.2 | async-start | bytes 8388608
  0.6 42.0 %slice-start.2 = ((s8[7340032]{0:T(1024)(128)(4,1)}), s8[4194304]{0:T(1024)(128)(4,1)S(1)}, s32[]{:S(2)}) async-start(s8[7340032]{0:T(1024)(128)(4,1)} %bitcast.15), calls=%async_computation.4 | async-start | bytes 8388608
  0.7 42.0 %slice-start.4 = ((s8[7340032]{0:T(1024)(128)(4,1)}), s8[4194304]{0:T(1024)(128)(4,1)S(1)}, s32[]{:S(2)}) async-start(s8[7340032]{0:T(1024)(128)(4,1)} %bitcast.18), calls=%async_computation.6 | async-start | bytes 8388608
  0.7 42.0 %slice-start.1 = ((s8[7340032]{0:T(1024)(128)(4,1)}), s8[3145728]{0:T(1024)(128)(4,1)S(1)}, s32[]{:S(2)}) async-start(s8[7340032]{0:T(1024)(128)(4,1)} %bitcast.12), calls=%async_computation.3 | async-start | bytes 6291456
  0.7 42.0 %slice-start.3 = ((s8[7340032]{0:T(1024)(128)(4,1)}), s8[3145728]{0:T(1024)(128)(4,1)S(1)}, s32[]{:S(2)}) async-start(s8[7340032]{0:T(1024)(128)(4,1)} %bitcast.15), calls=%async_computation.5 | async-start | bytes 6291456
  0.7 42.0 %slice-start.5 = ((s8[7340032]{0:T(1024)(128)(4,1)}), s8[3145728]{0:T(1024)(128)(4,1)S(1)}, s32[]{:S(2)}) async-start(s8[7340032]{0:T(1024)(128)(4,1)} %bitcast.18), calls=%async_computation.7 | async-start | bytes 6291456
  40.9 9.9 %collective-permute-start = (bf16[576,128]{1,0:T(8,128)(2,1)S(1)}, bf16[576,128]{1,0:T(8,128)(2,1)S(1)}, u32[]{:S(2)}, u32[]{:S(2)}) collective-permute-start(bf16[576,128]{1,0:T(8,128)(2,1)S(1)} %get-tuple-element.15), channel_id=1, source_target_pairs={{0,127},{1,0},{2,1},{3,2},{4,3},{5,4},{6,5},{7,6},{8,7},{9,8},{10,... | collective-permute-start | bytes 442376 | tf_op jit(solution)/shard_map/ppermute | solution.py:251
  50.8 4.9 %copy-start = (s32[384]{0:T(512)S(1)}, s32[384]{0:T(512)}, u32[]{:S(2)}) copy-start(s32[384]{0:T(512)} %source_hbm.3) | copy-start | bytes 4612
  50.8 4.9 %copy-start.1 = (s32[384]{0:T(512)S(1)}, s32[384]{0:T(512)}, u32[]{:S(2)}) copy-start(s32[384]{0:T(512)} %first_ref.3) | copy-start | bytes 4612
  50.8 4.9 %copy-start.2 = (s32[384]{0:T(512)S(1)}, s32[384]{0:T(512)}, u32[]{:S(2)}) copy-start(s32[384]{0:T(512)} %tokens_ref.3) | copy-start | bytes 4612
  50.8 9.1 %copy-start.3 = (s32[16,8]{0,1:T(8,128)S(1)}, s32[16,8]{0,1:T(8,128)}, u32[]{:S(2)}) copy-start(s32[16,8]{0,1:T(8,128)} %param.12) | copy-start | bytes 1540
  50.8 33.5 %all-to-all-start.1 = ((bf16[128,8,896]{2,1,0:T(8,128)(2,1)}), bf16[128,8,896]{2,1,0:T(8,128)(2,1)S(1)}, u32[]{:S(2)}, u32[]{:S(2)}) async-start(bf16[128,8,896]{2,1,0:T(8,128)(2,1)} %bitcast.24), calls=%async_computation.1 | async-start | bytes 3670016 | tf_op jit(solution)/shard_map/all_to_all | solution.py:248
  55.7 4.4 %copy-start.4 = (f32[16,8]{0,1:T(8,128)S(1)}, f32[16,8]{0,1:T(8,128)}, u32[]{:S(2)}) copy-start(f32[16,8]{0,1:T(8,128)} %param.13) | copy-start | bytes 1540
  58.8 25.5 %collective-permute-start.1 = (bf16[128,512]{1,0:T(8,128)(2,1)S(1)}, bf16[128,512]{1,0:T(8,128)(2,1)S(1)}, u32[]{:S(2)}, u32[]{:S(2)}) collective-permute-start(bf16[128,512]{1,0:T(8,128)(2,1)S(1)} %shard_map.125), channel_id=1, source_target_pairs={{0,1},{1,2},{2,3},{3,4},{4,5},{5,6},{6,7},{7,8},{8,9},{9,10},{10,1... | collective-permute-start | bytes 393224 | tf_op jit(solution)/shard_map/ppermute | solution.py:251
